TPU v7x, 32 devices: a whole 2x2x4 slice. The times are simulated.
32 devices in a mesh: shots: 2 (over x), depth: 8 (over z, y), freq: 2 (over core).
Axes of the slice: x: 2, y: 2, z: 4, core: 2. Of those that a mesh axis runs over, the one named last changes fastest.
Arguments:
- surface: float32 [2, 4, 2, 128, 256], P('shots', 'freq'), parts along dimension 0, may hold values from -2.1 to 2.1
- bins: int32 [8, 128, 128], P('depth'), may hold values from 0 to 7
- stencil: float32 [4, 8, 5], P('freq'), may hold values from 0.25 to 1
- phase_step: float32 [4, 8], P('freq'), may hold values from 0.3 to 1.4
- phase_shift: float32 [4, 8], P('freq'), may hold values from -3.140625 to 3.140625
- lags: int32 [4], replicated, may hold values from 0 to 7, as said below
Outputs:
- image: float32 [8, 8, 16384], P('depth', 'shots', 'freq'), parts along dimension 1
There are 2 independent parts, one for each index of `shots`. A program takes and returns all parts, laid end to end along the dimension named above; an argument that names none is the same for every part. Nothing has to cross between parts.
Inputs may be any that keep to these rules, and one draw needn't show every extreme that they name: `lags`: 4 distinct half-offsets in cells; one of them is 7.
All inputs are finite; a program needn't handle non-finite values.
Results may differ from a plain program's by a relative error of at most 0.0003.
Values sent between devices are 32-bit elements; how exact they have to be, the bound alone decides.
A program may use at most 64 MiB of HBM per device.

v0:
```python
import math

import jax
import jax.numpy as jnp
from jax import lax
from jax.sharding import PartitionSpec as P

KERNELS = 8
TAPS = 13
HALF = 6
LAGS = 4
HMAX = 7


column_tile = 16


def from_behind(value, axis, steps):
    count = lax.axis_size(axis)
    initial, last = (max(0, -steps), min(count, count - steps))
    return lax.ppermute(value, axis, [(source, source + steps) for source in range(initial, last)])


def kernel_taps(stencil, phase_step, phase_shift):
    center = stencil[..., 0]
    along_x = stencil[..., 1]
    along_y = stencil[..., 2]
    diag_main = stencil[..., 3]
    diag_anti = stencil[..., 4]
    row_above = jnp.stack([diag_main, along_y, diag_anti], -1)
    row_middle = jnp.stack([along_x, center, along_x], -1)
    row_below = jnp.stack([diag_anti, along_y, diag_main], -1)
    stencil_grid = jnp.stack([row_above, row_middle, row_below], -2)
    weight_sum = center + 2.0 * (along_x + along_y + diag_main + diag_anti)
    stencil_grid = stencil_grid * (phase_step / weight_sum)[..., None, None]
    lead = stencil.shape[:-1]
    tap_rows = lax.broadcasted_iota(jnp.int32, (TAPS, TAPS), 0)
    tap_cols = lax.broadcasted_iota(jnp.int32, (TAPS, TAPS), 1)
    unit_tap = ((tap_rows == HALF) & (tap_cols == HALF)).astype(jnp.float32)
    power = jnp.broadcast_to(unit_tap, lead + (TAPS, TAPS))
    real_sum = power
    imag_sum = jnp.zeros(lead + (TAPS, TAPS), jnp.float32)
    pad_spec = [(0, 0)] * len(lead) + [(1, 1), (1, 1)]
    for order in range(1, HALF + 1):
        padded = jnp.pad(power, pad_spec)
        grown = jnp.zeros(lead + (TAPS, TAPS), jnp.float32)
        for row_off in range(3):
            for col_off in range(3):
                piece = padded[
                    ..., 2 - row_off : 2 - row_off + TAPS, 2 - col_off : 2 - col_off + TAPS
                ]
                grown = grown + stencil_grid[..., row_off, col_off, None, None] * piece
        power = grown
        weighted = power * (1.0 / math.factorial(order))
        if order % 4 == 1:
            imag_sum = imag_sum + weighted
        elif order % 4 == 2:
            real_sum = real_sum - weighted
        elif order % 4 == 3:
            imag_sum = imag_sum - weighted
        else:
            real_sum = real_sum + weighted
    cosine = jnp.cos(phase_shift)[..., None, None]
    sine = jnp.sin(phase_shift)[..., None, None]
    return (cosine * real_sum - sine * imag_sum, sine * real_sum + cosine * imag_sum)


def advance_level(fields, weights, selector):
    field_count = fields.shape[0]
    grid_width = fields.shape[1]
    tiles = grid_width // column_tile
    parts = fields.reshape(field_count, grid_width, 2, grid_width)
    padded = jnp.pad(parts, ((0, 0), (HALF, HALF), (0, 0), (HALF, column_tile - HALF)))
    main = padded[..., :grid_width].reshape(
        field_count, grid_width + 2 * HALF, 2, tiles, column_tile
    )
    after = padded[..., column_tile : grid_width + column_tile].reshape(
        field_count, grid_width + 2 * HALF, 2, tiles, column_tile
    )
    windows = jnp.concatenate([main, after[..., : 2 * HALF]], -1)
    windows = jnp.transpose(windows, (0, 1, 3, 2, 4))
    patches = jnp.stack(
        [windows[:, row_tap : row_tap + grid_width] for row_tap in range(TAPS)], axis=3
    )
    patches = patches.reshape(field_count * grid_width * tiles, TAPS * 2 * (column_tile + 2 * HALF))
    result = jnp.dot(
        patches, weights, precision=lax.Precision.HIGHEST, preferred_element_type=jnp.float32
    )
    result = result.reshape(field_count, grid_width, tiles, KERNELS, 2, column_tile)
    chosen = jnp.sum(result * selector[None], axis=3)
    return jnp.transpose(chosen, (0, 1, 3, 2, 4)).reshape(field_count, grid_width, 2 * grid_width)


def image_terms(source, receiver, lags):
    grid_width = source.shape[0]
    source_parts = jnp.pad(
        source.reshape(grid_width, 2, grid_width), ((0, 0), (0, 0), (HMAX, HMAX))
    )
    receiver_parts = jnp.pad(
        receiver.reshape(grid_width, 2, grid_width), ((0, 0), (0, 0), (HMAX, HMAX))
    )
    lag_terms = []
    for lag_index in range(LAGS):
        offset = lags[lag_index]
        shifted_source = lax.dynamic_slice_in_dim(source_parts, HMAX - offset, grid_width, 2)
        shifted_receiver = lax.dynamic_slice_in_dim(receiver_parts, HMAX + offset, grid_width, 2)
        lag_terms.append(jnp.sum(shifted_source * shifted_receiver, axis=1))
    return jnp.stack(lag_terms)


def body(surface, bins, stencil, phase_step, phase_shift, lags):
    shot_count = surface.shape[0]
    freq_count = surface.shape[1]
    grid_width = surface.shape[3]
    slab_steps = bins.shape[0]
    tiles = grid_width // column_tile
    window_width = column_tile + 2 * HALF
    depth_count = lax.axis_size("depth")
    depth_index = lax.axis_index("depth")
    kern_real, kern_imag = kernel_taps(stencil, phase_step, phase_shift)
    mixing = jnp.stack(
        [jnp.stack([kern_real, kern_imag], 1), jnp.stack([-kern_imag, kern_real], 1)], 1
    )
    window_ids = lax.broadcasted_iota(jnp.int32, (window_width, column_tile, TAPS), 0)
    out_ids = lax.broadcasted_iota(jnp.int32, (window_width, column_tile, TAPS), 1)
    tap_ids = lax.broadcasted_iota(jnp.int32, (window_width, column_tile, TAPS), 2)
    shift_table = (window_ids == out_ids + tap_ids).astype(jnp.float32)
    all_weights = jnp.einsum(
        "fpqkab,cwb->fapckqw", mixing, shift_table, precision=lax.Precision.HIGHEST
    )
    all_weights = all_weights.reshape(
        freq_count, TAPS * 2 * window_width, KERNELS * 2 * column_tile
    )
    kernel_ids = lax.broadcasted_iota(jnp.int32, (1, 1, 1, KERNELS, 1, 1), 3)
    selectors = (
        bins.reshape(slab_steps, grid_width, tiles, 1, 1, column_tile) == kernel_ids
    ).astype(jnp.float32)
    image_part = jnp.zeros((slab_steps, LAGS, grid_width, grid_width), jnp.float32)
    front_count = shot_count * freq_count

    def advance_turn(step_index, carry):
        sent, image_now = carry
        received = from_behind(sent, "depth", 1)
        front_index = step_index - depth_index
        active = (front_index >= 0) & (front_index < front_count)
        clipped = jnp.clip(front_index, 0, front_count - 1)
        shot_index = clipped // freq_count
        freq_index = clipped % freq_count
        shot_fields = lax.dynamic_index_in_dim(surface, shot_index, 0, keepdims=False)
        surface_front = lax.dynamic_index_in_dim(shot_fields, freq_index, 0, keepdims=False)
        incoming = jnp.where(depth_index == 0, surface_front, received)
        weights_front = lax.dynamic_index_in_dim(all_weights, freq_index, 0, keepdims=False)

        def compute_front(state):
            fields, image_held = state
            fields = advance_level(fields, weights_front, selectors[0])
            level_terms = [image_terms(fields[0], fields[1], lags)]
            return (fields, image_held + jnp.stack(level_terms))

        def keep_state(state):
            return state

        return lax.cond(active, compute_front, keep_state, (incoming, image_now))

    start = (jnp.zeros((2, grid_width, 2 * grid_width), jnp.float32), image_part)
    final_sent, image_part = lax.fori_loop(0, depth_count + front_count - 1, advance_turn, start)
    image_part = image_part.reshape(slab_steps, LAGS, grid_width * grid_width)
    return lax.psum_scatter(image_part, "freq", scatter_dimension=2, tiled=True)


def solution(mesh):
    return jax.shard_map(
        body,
        mesh=mesh,
        in_specs=(
            P("shots", "freq", None, None, None),
            P("depth", None, None),
            P("freq", None, None),
            P("freq", None),
            P("freq", None),
            P(),
        ),
        out_specs=P("depth", "shots", "freq"),
        check_vma=False,
    )
```

profile of v0, /device:TPU:0, one launch (start us, length us, event | category | flops | bytes accessed | tf_op | source)
XLA Modules:
  0.0 383.8 jit_solution(565116637435025677)
XLA Ops:
  6.5 0.7 fusion.78
  7.3 0.7 fusion.79
  8.0 0.8 bitcast_divide_fusion
  8.9 0.4 fusion.39
  9.3 0.4 multiply_add_fusion.5
  9.7 0.4 multiply_add_fusion.4
  10.2 0.4 multiply_add_fusion.3
  10.6 0.4 multiply_add_fusion.2
  11.0 0.7 fusion.80
  11.8 1.1 fusion.74
  13.0 5.6 %convolution_bitcast_fusion = f32[2,13,2,28,8,2,16]{3,1,4,5,2,0,6:T(8,128)} fusion(f32[2,1,2,8,13,13]{5,4,3,2,1,0:T(8,128)S(1)} %get-tuple-element.337, f32[2,1,2,8,13,13]{5,4,3,2,1,0:T(8,128)S(1)} %get-tuple-element.336), kind=kOutput, calls=%fused_computation.56 | convolution fusion | flops 58169280 | bytes 1534208 | tf_op jit(solution)/shard_map/fpqkab,cwb->fapckqw/dot_general | solution.py:128
  18.6 11.5 %copy.36 = f32[2,13,2,28,8,2,16]{3,2,1,6,5,4,0:T(2,128)} copy(f32[2,13,2,28,8,2,16]{3,1,4,5,2,0,6:T(8,128)} %convolution_bitcast_fusion) | data formatting | bytes 2981888 | tf_op jit(solution)/shard_map/fpqkab,cwb->fapckqw/transpose | solution.py:128
  30.1 6.1 %reshape.91 = f32[2,728,256]{1,2,0:T(8,128)S(1)} reshape(f32[2,13,2,28,8,2,16]{3,2,1,6,5,4,0:T(2,128)} %copy.36) | data formatting | bytes 2981888 | tf_op jit(solution)/shard_map/reshape | solution.py:131
  36.5 208.1 %while.18 = (s32[]{:T(128)}, f32[2,128,256]{1,2,0:T(8,128)S(1)}, f32[1,4,128,128]{2,3,1,0:T(8,128)S(1)}, s32[]{:T(128)}, pred[]{:T(512)}, /*index=5*/f32[1,2,2,1...) while((s32[]{:T(128)}, f32[2,128,256]{1,2,0:T(8,128)S(1)}, ...), condition=%wide.region_8.9_spmd.clone, body=%wide.region_0.8_spmd.clone.sunk | while | flops 4582074880 | bytes 42677048 | solution.py:166
  36.6 4.9 %collective-permute-start = (f32[2,128,256]{1,2,0:T(8,128)S(1)}, f32[2,128,256]{1,2,0:T(8,128)S(1)}, u32[]{:S(2)}, u32[]{:S(2)}) collective-permute-start(f32[2,128,256]{1,2,0:T(8,128)S(1)} %get-tuple-element.434), channel_id=1, source_target_pairs={{0,2},{2,4},{4,6},{6,8},{8,10},{10,12},{12,14},{1,3},{3,5},{5,7},{... | collective-permute-start | bytes 786440 | tf_op jit(solution)/shard_map/while/body/eval_jaxpr/ppermute | solution.py:21
  41.8 5.3 %collective-permute-done = f32[2,128,256]{1,2,0:T(8,128)S(1)} collective-permute-done((f32[2,128,256]{1,2,0:T(8,128)S(1)}, f32[2,128,256]{1,2,0:T(8,128)S(1)}, u32[]{:S(2)}, u32[]{:S(2)}) %collective-permute-start) | collective-permute-done | bytes 262176 | tf_op jit(solution)/shard_map/while/body/eval_jaxpr/ppermute | solution.py:21
  47.1 26.1 %conditional.3 = ((f32[2,128,256]{1,2,0:T(8,128)S(1)}, f32[1,4,128,128]{2,3,1,0:T(8,128)S(1)})) conditional(s32[]{:T(128)} %convert_element_type.53, (f32[2,128,256]{1,2,0:T(8,128)S(1)}, f32[1,4,128,128]{2,3,1,0:T(8,128)S(1)}) %tuple.81, (f32[2,128,256]{1,2,0:T(8,128)S(1)}, f32[2,728,256]{1,2,0:T(8,128)S(1)}, s32[]{:T(128)}, ...), branch_computations={%region_1.1_spmd, %region_2.7_spmd} | conditional | flops 4581747200 | bytes 39203260 | solution.py:163
  47.1 0.3 pad_slice_fusion.1
  47.8 0.2 fusion.16
  48.0 0.2 fusion.15
  48.8 0.2 fusion.11
  50.1 5.7 %copy.29 = f32[2,128,8,13,2,28]{1,2,5,4,3,0:T(8,128)S(1)} copy(f32[2,128,8,13,2,28]{1,5,2,4,0,3:T(8,128)S(1)} %fusion.6) | data formatting | bytes 11927552 | tf_op jit(solution)/shard_map/while/body/eval_jaxpr/cond/branch_1_fun/stack | solution.py:82
  55.8 6.3 %multiply_reduce_fusion = f32[2,128,8,2,16]{1,4,3,2,0:T(8,128)S(1)} fusion(f32[8,2,16,728,1,1]{3,2,1,0,5,4:T(8,128)S(1)} %bitcast.171, f32[2,128,8,728,1,1]{1,2,3,0,5,4:T(8,128)S(1)} %bitcast.165, f32[128,8,8,16]{0,3,2,1:T(8,128)S(1)} %bitcast.172), kind=kOutput, calls=%fused_computation.3 | convolution fusion | flops 4581163008 | bytes 7495680 | tf_op jit(solution)/shard_map/while/body/eval_jaxpr/cond/branch_1_fun/dot_general | solution.py:86
  62.2 0.7 fusion.77
  73.2 1.3 collective-permute-start
  74.8 4.7 %collective-permute-done = f32[2,128,256]{1,2,0:T(8,128)S(1)} collective-permute-done((f32[2,128,256]{1,2,0:T(8,128)S(1)}, f32[2,128,256]{1,2,0:T(8,128)S(1)}, u32[]{:S(2)}, u32[]{:S(2)}) %collective-permute-start) | collective-permute-done | bytes 262176 | tf_op jit(solution)/shard_map/while/body/eval_jaxpr/ppermute | solution.py:21
  79.5 26.1 %conditional.3 = ((f32[2,128,256]{1,2,0:T(8,128)S(1)}, f32[1,4,128,128]{2,3,1,0:T(8,128)S(1)})) conditional(s32[]{:T(128)} %convert_element_type.53, (f32[2,128,256]{1,2,0:T(8,128)S(1)}, f32[1,4,128,128]{2,3,1,0:T(8,128)S(1)}) %tuple.81, (f32[2,128,256]{1,2,0:T(8,128)S(1)}, f32[2,728,256]{1,2,0:T(8,128)S(1)}, s32[]{:T(128)}, ...), branch_computations={%region_1.1_spmd, %region_2.7_spmd} | conditional | flops 4581747200 | bytes 39203260 | solution.py:163
  79.5 0.3 pad_slice_fusion.1
  82.4 5.7 %copy.29 = f32[2,128,8,13,2,28]{1,2,5,4,3,0:T(8,128)S(1)} copy(f32[2,128,8,13,2,28]{1,5,2,4,0,3:T(8,128)S(1)} %fusion.6) | data formatting | bytes 11927552 | tf_op jit(solution)/shard_map/while/body/eval_jaxpr/cond/branch_1_fun/stack | solution.py:82
  88.2 6.3 %multiply_reduce_fusion = f32[2,128,8,2,16]{1,4,3,2,0:T(8,128)S(1)} fusion(f32[8,2,16,728,1,1]{3,2,1,0,5,4:T(8,128)S(1)} %bitcast.171, f32[2,128,8,728,1,1]{1,2,3,0,5,4:T(8,128)S(1)} %bitcast.165, f32[128,8,8,16]{0,3,2,1:T(8,128)S(1)} %bitcast.172), kind=kOutput, calls=%fused_computation.3 | convolution fusion | flops 4581163008 | bytes 7495680 | tf_op jit(solution)/shard_map/while/body/eval_jaxpr/cond/branch_1_fun/dot_general | solution.py:86
  94.6 0.7 fusion.77
  105.6 4.4 %collective-permute-start = (f32[2,128,256]{1,2,0:T(8,128)S(1)}, f32[2,128,256]{1,2,0:T(8,128)S(1)}, u32[]{:S(2)}, u32[]{:S(2)}) collective-permute-start(f32[2,128,256]{1,2,0:T(8,128)S(1)} %get-tuple-element.434), channel_id=1, source_target_pairs={{0,2},{2,4},{4,6},{6,8},{8,10},{10,12},{12,14},{1,3},{3,5},{5,7},{... | collective-permute-start | bytes 786440 | tf_op jit(solution)/shard_map/while/body/eval_jaxpr/ppermute | solution.py:21
  110.2 3.8 collective-permute-done
  114.1 30.5 %collective-permute-start = (f32[2,128,256]{1,2,0:T(8,128)S(1)}, f32[2,128,256]{1,2,0:T(8,128)S(1)}, u32[]{:S(2)}, u32[]{:S(2)}) collective-permute-start(f32[2,128,256]{1,2,0:T(8,128)S(1)} %get-tuple-element.434), channel_id=1, source_target_pairs={{0,2},{2,4},{4,6},{6,8},{8,10},{10,12},{12,14},{1,3},{3,5},{5,7},{... | collective-permute-start | bytes 786440 | tf_op jit(solution)/shard_map/while/body/eval_jaxpr/ppermute | solution.py:21
  144.8 3.6 collective-permute-done
  148.5 4.4 %collective-permute-start = (f32[2,128,256]{1,2,0:T(8,128)S(1)}, f32[2,128,256]{1,2,0:T(8,128)S(1)}, u32[]{:S(2)}, u32[]{:S(2)}) collective-permute-start(f32[2,128,256]{1,2,0:T(8,128)S(1)} %get-tuple-element.434), channel_id=1, source_target_pairs={{0,2},{2,4},{4,6},{6,8},{8,10},{10,12},{12,14},{1,3},{3,5},{5,7},{... | collective-permute-start | bytes 786440 | tf_op jit(solution)/shard_map/while/body/eval_jaxpr/ppermute | solution.py:21
  153.1 3.6 collective-permute-done
  156.8 30.1 %collective-permute-start = (f32[2,128,256]{1,2,0:T(8,128)S(1)}, f32[2,128,256]{1,2,0:T(8,128)S(1)}, u32[]{:S(2)}, u32[]{:S(2)}) collective-permute-start(f32[2,128,256]{1,2,0:T(8,128)S(1)} %get-tuple-element.434), channel_id=1, source_target_pairs={{0,2},{2,4},{4,6},{6,8},{8,10},{10,12},{12,14},{1,3},{3,5},{5,7},{... | collective-permute-start | bytes 786440 | tf_op jit(solution)/shard_map/while/body/eval_jaxpr/ppermute | solution.py:21
  187.1 3.6 collective-permute-done
  190.8 5.3 %collective-permute-start = (f32[2,128,256]{1,2,0:T(8,128)S(1)}, f32[2,128,256]{1,2,0:T(8,128)S(1)}, u32[]{:S(2)}, u32[]{:S(2)}) collective-permute-start(f32[2,128,256]{1,2,0:T(8,128)S(1)} %get-tuple-element.434), channel_id=1, source_target_pairs={{0,2},{2,4},{4,6},{6,8},{8,10},{10,12},{12,14},{1,3},{3,5},{5,7},{... | collective-permute-start | bytes 786440 | tf_op jit(solution)/shard_map/while/body/eval_jaxpr/ppermute | solution.py:21
  196.4 3.6 collective-permute-done
  200.1 29.7 %collective-permute-start = (f32[2,128,256]{1,2,0:T(8,128)S(1)}, f32[2,128,256]{1,2,0:T(8,128)S(1)}, u32[]{:S(2)}, u32[]{:S(2)}) collective-permute-start(f32[2,128,256]{1,2,0:T(8,128)S(1)} %get-tuple-element.434), channel_id=1, source_target_pairs={{0,2},{2,4},{4,6},{6,8},{8,10},{10,12},{12,14},{1,3},{3,5},{5,7},{... | collective-permute-start | bytes 786440 | tf_op jit(solution)/shard_map/while/body/eval_jaxpr/ppermute | solution.py:21
  230.0 6.2 %collective-permute-done = f32[2,128,256]{1,2,0:T(8,128)S(1)} collective-permute-done((f32[2,128,256]{1,2,0:T(8,128)S(1)}, f32[2,128,256]{1,2,0:T(8,128)S(1)}, u32[]{:S(2)}, u32[]{:S(2)}) %collective-permute-start) | collective-permute-done | bytes 262176 | tf_op jit(solution)/shard_map/while/body/eval_jaxpr/ppermute | solution.py:21
  236.3 4.4 %collective-permute-start = (f32[2,128,256]{1,2,0:T(8,128)S(1)}, f32[2,128,256]{1,2,0:T(8,128)S(1)}, u32[]{:S(2)}, u32[]{:S(2)}) collective-permute-start(f32[2,128,256]{1,2,0:T(8,128)S(1)} %get-tuple-element.434), channel_id=1, source_target_pairs={{0,2},{2,4},{4,6},{6,8},{8,10},{10,12},{12,14},{1,3},{3,5},{5,7},{... | collective-permute-start | bytes 786440 | tf_op jit(solution)/shard_map/while/body/eval_jaxpr/ppermute | solution.py:21
  240.9 3.6 collective-permute-done
  244.6 7.7 %copy.47 = f32[1,4,128,128]{1,3,2,0:T(8,128)} copy(f32[1,4,128,128]{2,3,1,0:T(8,128)S(1)} %get-tuple-element.259) | data formatting | bytes 524288
  252.3 116.0 %reduce-scatter.4.cloned.1.call-done = f32[8192,4]{1,0:T(8,128)} async-done(((f32[16384,4]{1,0:T(8,128)}), f32[8192,4]{1,0:T(8,128)}) %reduce-scatter.4.cloned.1.call-update) | async-done | bytes 131088
  368.3 8.6 %copy.46 = f32[1,4,8192]{2,1,0:T(4,128)} copy(f32[1,4,8192]{1,0,2:T(1,128)} %bitcast.181) | data formatting | bytes 262144
  (101 shorter events, 7.7 us)
Async XLA Ops:
  6.5 361.7 %reduce-scatter.4.cloned.1.call-start = ((), (), s32[]{:S(2)}) async-start(), calls=%async_computation.1 | async-start | bytes 12582912
  30.1 6.1 %copy-start.2 = (s32[1,128,128]{2,1,0:T(8,128)S(1)}, s32[1,128,128]{2,1,0:T(8,128)}, u32[]{:S(2)}) copy-start(s32[1,128,128]{2,1,0:T(8,128)} %param.11) | copy-start | bytes 196612
  30.1 6.3 %copy-start = (f32[1,2,2,128,256]{4,3,2,1,0:T(8,128)S(1)}, f32[1,2,2,128,256]{4,3,2,1,0:T(8,128)}, u32[]{:S(2)}) copy-start(f32[1,2,2,128,256]{4,3,2,1,0:T(8,128)} %param.10) | copy-start | bytes 1572868
  30.1 6.3 %copy-start.1 = (s32[4]{0:T(128)S(1)}, s32[4]{0:T(128)}, u32[]{:S(2)}) copy-start(s32[4]{0:T(128)} %param.15) | copy-start | bytes 52
  36.6 10.4 %collective-permute-start = (f32[2,128,256]{1,2,0:T(8,128)S(1)}, f32[2,128,256]{1,2,0:T(8,128)S(1)}, u32[]{:S(2)}, u32[]{:S(2)}) collective-permute-start(f32[2,128,256]{1,2,0:T(8,128)S(1)} %get-tuple-element.434), channel_id=1, source_target_pairs={{0,2},{2,4},{4,6},{6,8},{8,10},{10,12},{12,14},{1,3},{3,5},{5,7},{... | collective-permute-start | bytes 786440 | tf_op jit(solution)/shard_map/while/body/eval_jaxpr/ppermute | solution.py:21
  73.2 6.2 %collective-permute-start = (f32[2,128,256]{1,2,0:T(8,128)S(1)}, f32[2,128,256]{1,2,0:T(8,128)S(1)}, u32[]{:S(2)}, u32[]{:S(2)}) collective-permute-start(f32[2,128,256]{1,2,0:T(8,128)S(1)} %get-tuple-element.434), channel_id=1, source_target_pairs={{0,2},{2,4},{4,6},{6,8},{8,10},{10,12},{12,14},{1,3},{3,5},{5,7},{... | collective-permute-start | bytes 786440 | tf_op jit(solution)/shard_map/while/body/eval_jaxpr/ppermute | solution.py:21
  105.6 8.4 %collective-permute-start = (f32[2,128,256]{1,2,0:T(8,128)S(1)}, f32[2,128,256]{1,2,0:T(8,128)S(1)}, u32[]{:S(2)}, u32[]{:S(2)}) collective-permute-start(f32[2,128,256]{1,2,0:T(8,128)S(1)} %get-tuple-element.434), channel_id=1, source_target_pairs={{0,2},{2,4},{4,6},{6,8},{8,10},{10,12},{12,14},{1,3},{3,5},{5,7},{... | collective-permute-start | bytes 786440 | tf_op jit(solution)/shard_map/while/body/eval_jaxpr/ppermute | solution.py:21
  114.1 34.3 %collective-permute-start = (f32[2,128,256]{1,2,0:T(8,128)S(1)}, f32[2,128,256]{1,2,0:T(8,128)S(1)}, u32[]{:S(2)}, u32[]{:S(2)}) collective-permute-start(f32[2,128,256]{1,2,0:T(8,128)S(1)} %get-tuple-element.434), channel_id=1, source_target_pairs={{0,2},{2,4},{4,6},{6,8},{8,10},{10,12},{12,14},{1,3},{3,5},{5,7},{... | collective-permute-start | bytes 786440 | tf_op jit(solution)/shard_map/while/body/eval_jaxpr/ppermute | solution.py:21
  148.5 8.3 %collective-permute-start = (f32[2,128,256]{1,2,0:T(8,128)S(1)}, f32[2,128,256]{1,2,0:T(8,128)S(1)}, u32[]{:S(2)}, u32[]{:S(2)}) collective-permute-start(f32[2,128,256]{1,2,0:T(8,128)S(1)} %get-tuple-element.434), channel_id=1, source_target_pairs={{0,2},{2,4},{4,6},{6,8},{8,10},{10,12},{12,14},{1,3},{3,5},{5,7},{... | collective-permute-start | bytes 786440 | tf_op jit(solution)/shard_map/while/body/eval_jaxpr/ppermute | solution.py:21
  156.8 33.9 %collective-permute-start = (f32[2,128,256]{1,2,0:T(8,128)S(1)}, f32[2,128,256]{1,2,0:T(8,128)S(1)}, u32[]{:S(2)}, u32[]{:S(2)}) collective-permute-start(f32[2,128,256]{1,2,0:T(8,128)S(1)} %get-tuple-element.434), channel_id=1, source_target_pairs={{0,2},{2,4},{4,6},{6,8},{8,10},{10,12},{12,14},{1,3},{3,5},{5,7},{... | collective-permute-start | bytes 786440 | tf_op jit(solution)/shard_map/while/body/eval_jaxpr/ppermute | solution.py:21
  190.8 9.2 %collective-permute-start = (f32[2,128,256]{1,2,0:T(8,128)S(1)}, f32[2,128,256]{1,2,0:T(8,128)S(1)}, u32[]{:S(2)}, u32[]{:S(2)}) collective-permute-start(f32[2,128,256]{1,2,0:T(8,128)S(1)} %get-tuple-element.434), channel_id=1, source_target_pairs={{0,2},{2,4},{4,6},{6,8},{8,10},{10,12},{12,14},{1,3},{3,5},{5,7},{... | collective-permute-start | bytes 786440 | tf_op jit(solution)/shard_map/while/body/eval_jaxpr/ppermute | solution.py:21
  200.1 36.1 %collective-permute-start = (f32[2,128,256]{1,2,0:T(8,128)S(1)}, f32[2,128,256]{1,2,0:T(8,128)S(1)}, u32[]{:S(2)}, u32[]{:S(2)}) collective-permute-start(f32[2,128,256]{1,2,0:T(8,128)S(1)} %get-tuple-element.434), channel_id=1, source_target_pairs={{0,2},{2,4},{4,6},{6,8},{8,10},{10,12},{12,14},{1,3},{3,5},{5,7},{... | collective-permute-start | bytes 786440 | tf_op jit(solution)/shard_map/while/body/eval_jaxpr/ppermute | solution.py:21
  236.3 8.3 %collective-permute-start = (f32[2,128,256]{1,2,0:T(8,128)S(1)}, f32[2,128,256]{1,2,0:T(8,128)S(1)}, u32[]{:S(2)}, u32[]{:S(2)}) collective-permute-start(f32[2,128,256]{1,2,0:T(8,128)S(1)} %get-tuple-element.434), channel_id=1, source_target_pairs={{0,2},{2,4},{4,6},{6,8},{8,10},{10,12},{12,14},{1,3},{3,5},{5,7},{... | collective-permute-start | bytes 786440 | tf_op jit(solution)/shard_map/while/body/eval_jaxpr/ppermute | solution.py:21
Sparse Core Ops, SparseCore 0:
  252.4 115.8 reduce-scatter.3
where the time goes:
time: 385 us; the launch traced here: 384 us
  waiting for transfers between devices  154 us (40%)
  starting transfers between devices  115 us (30%)
  local copies, waits for them, and re-layouts  56.1 us (15%)
  loops' own time  21.4 us (6%)
  matrix products  18.3 us (5%)
  between operations  13.5 us (4%)
  other arithmetic  5.48 us (1%)
    unnamed x2, waiting for transfers between devices  116 us
    ppermute x9, starting transfers between devices, from_behind(): lax.ppermute(value, axis, [(source, source + steps) for source in range(i...  115 us
    ppermute x9, waiting for transfers between devices, from_behind(): lax.ppermute(value, axis, [(source, source + steps) for source in range(i...  38.1 us
    another operation x9, loops' own time, advance_turn(): return lax.cond(active, compute_front, keep_state, (incoming, image_now))  20.5 us
    unnamed x9, local copies, waits for them, and re-layouts  16.4 us
    dot_general x2, matrix products, advance_level(): jnp.dot(patches, weights, precision=lax.Precision.HIGHEST, preferred_elem...  12.6 us
    another operation x4, local copies, waits for them, and re-layouts, advance_level(): jnp.stack([windows[:, row_tap:row_tap + grid_width] for row_tap in range(...  11.8 us
    transpose x1, local copies, waits for them, and re-layouts, body(): jnp.einsum('fpqkab,cwb->fapckqw', mixing, shift_table, precision=lax.Prec...  11.5 us
  transfers between devices with their start and end apart: 10, of which 10 were waited for; matrix products, arithmetic and copies ran while one was open for 0% of the time, Pallas kernels for 0%

commit v1 on v0

v1 whole, which is shorter than its diff:
```python
import functools
import math

import jax
import jax.numpy as jnp
from jax import lax
from jax.experimental import pallas as pl
from jax.experimental.pallas import tpu as pltpu
from jax.sharding import PartitionSpec as P

HALF = 6
TAPS = 2 * HALF + 1
HALO = 8
ROWS = 16
WINDOW = ROWS + 2 * HALO
PARTS = 4
LANES = 128
PER_TILE = LANES // WINDOW
MAIN = (TAPS // PER_TILE) * LANES
CONTRACT = 3 * MAIN + LANES
MESH = pl.DeviceIdType.MESH


def snake(index):
    pair = index // 2
    return 2 * pair + (index % 2 + pair % 2) % 2


def column(row_values, count):
    rows = lax.broadcasted_iota(jnp.int32, (count, count), 0)
    cols = lax.broadcasted_iota(jnp.int32, (count, count), 1)
    spread = jnp.broadcast_to(row_values, (count, count))
    return jnp.sum(jnp.where(rows == cols, spread, 0.0), axis=1, keepdims=True)


def build_taps(weights, step, shift, kernels):
    center, along_x, along_y, main, anti = (weights[:, j : j + 1] for j in range(5))
    scale = step / (center + 2.0 * (along_x + along_y + main + anti))
    center, along_x, along_y, main, anti = (
        jnp.broadcast_to(part * scale, (kernels, LANES))
        for part in (center, along_x, along_y, main, anti)
    )
    lane = lax.broadcasted_iota(jnp.int32, (kernels, LANES), 1)
    tiles = -(-TAPS // PER_TILE)
    zero = jnp.zeros((kernels, LANES), jnp.float32)
    power = [zero for _ in range(tiles)]
    spot = (HALF % PER_TILE) * WINDOW + HALO
    power[HALF // PER_TILE] = jnp.where(lane == spot, 1.0, 0.0)
    real = list(power)
    imag = [zero for _ in range(tiles)]
    for order in range(1, HALF + 1):
        right = [pltpu.roll(tile, WINDOW, 1) for tile in power]
        left = [pltpu.roll(tile, LANES - WINDOW, 1) for tile in power]
        grown = []
        for t in range(tiles):
            before = jnp.where(lane < WINDOW, right[t - 1] if t else zero, right[t])
            after = jnp.where(
                lane >= LANES - WINDOW, left[t + 1] if t + 1 < tiles else zero, left[t]
            )
            tall = along_y * power[t]
            down = tall + main * before + anti * after
            up = tall + main * after + anti * before
            flat = center * power[t] + along_x * (before + after)
            grown.append(flat + pltpu.roll(down, 1, 1) + pltpu.roll(up, LANES - 1, 1))
        power = grown
        sign = 1.0 if order % 4 < 2 else -1.0
        factor = sign / math.factorial(order)
        target = imag if order % 2 else real
        for t in range(tiles):
            target[t] = target[t] + power[t] * factor
    cosine = jnp.broadcast_to(jnp.cos(shift), (kernels, LANES))
    sine = jnp.broadcast_to(jnp.sin(shift), (kernels, LANES))
    kern_real = [cosine * r - sine * i for r, i in zip(real, imag)]
    kern_imag = [sine * r + cosine * i for r, i in zip(real, imag)]
    return kern_real, kern_imag


def split(value):
    high = value.astype(jnp.bfloat16)
    low = (value - high.astype(jnp.float32)).astype(jnp.bfloat16)
    return high, low


def kernel(
    depth, groups, freqs,
    surface, bins, stencil, phase_step, phase_shift, lags, out,
    field, level_bins, spread, taps, patches, part, mirror, total,
    bins_send, bins_recv, halo_send, halo_recv, swap_send, swap_recv, out_send, out_recv,
):
    freq_count = surface.shape[1]
    kernels = stencil.shape[1]
    width = surface.shape[4] // 2
    lag_count = lags.shape[0]
    strips = depth // groups
    share = lag_count // freqs
    per_core = strips // freqs
    here = lax.axis_index("depth")
    core = lax.axis_index("freq")
    group = here // strips
    strip = snake(here % strips)
    has_up = strip > 0
    has_down = strip < strips - 1

    field[...] = jnp.zeros_like(field)
    first = pl.multiple_of(strip * ROWS, ROWS)
    for f in range(freq_count):
        for j in range(PARTS):
            cols = pl.ds((j % 2) * width, width)
            field[0, f, j, pl.ds(HALO, ROWS), :] = surface[0, f, j // 2, pl.ds(first, ROWS), cols]

            @pl.when(has_up)
            def _():
                above = pl.multiple_of(jnp.maximum(first - HALO, 0), HALO)
                field[0, f, j, pl.ds(0, HALO), :] = surface[0, f, j // 2, pl.ds(above, HALO), cols]

            @pl.when(has_down)
            def _():
                below = pl.multiple_of(jnp.minimum(first + ROWS, (strips - 1) * ROWS), HALO)
                field[0, f, j, pl.ds(HALO + ROWS, HALO), :] = surface[
                    0, f, j // 2, pl.ds(below, HALO), cols
                ]

    barrier = pltpu.get_barrier_semaphore()

    def greet(step, carry):
        other = (here * freqs + core + step) % (depth * freqs)
        pl.semaphore_signal(
            barrier, inc=1, device_id={"depth": other // freqs, "freq": other % freqs},
            device_id_type=MESH,
        )
        return carry

    lax.fori_loop(1, depth * freqs, greet, 0)

    level_bins[here] = bins[0, pl.ds(first, ROWS), :]
    for f in range(freq_count):
        patches[f, 3 * MAIN + 3 * WINDOW :, :] = jnp.zeros((WINDOW, PARTS * width), jnp.bfloat16)
        step = column(phase_step[f : f + 1, :], kernels)
        shift = column(phase_shift[f : f + 1, :], kernels)
        kern = build_taps(stencil[f], step, shift, kernels)
        for c in range(2):
            for t in range(len(kern[c])):
                for y in range(ROWS):
                    moved = pltpu.roll(kern[c][t], y, 1) if y else kern[c][t]
                    spread[f, t, pl.ds(c * ROWS + y, kernels, stride=2 * ROWS), :] = moved
        for t in range(MAIN // LANES):
            high, low = split(spread[f, t])
            taps[f, :, t * LANES : (t + 1) * LANES] = high
            taps[f, :, MAIN + t * LANES : MAIN + (t + 1) * LANES] = high
            taps[f, :, 2 * MAIN + t * LANES : 2 * MAIN + (t + 1) * LANES] = low
        high, low = split(spread[f, MAIN // LANES])
        high, low = high.astype(jnp.float32), low.astype(jnp.float32)
        last = high + pltpu.roll(high, WINDOW, 1) + pltpu.roll(low, 2 * WINDOW, 1)
        taps[f, :, 3 * MAIN :] = last.astype(jnp.bfloat16)

    pl.semaphore_wait(barrier, depth * freqs - 1)

    def bins_copy(target, level, sem):
        rows = pl.ds(pl.multiple_of(snake(target % strips) * ROWS, ROWS), ROWS)
        return pltpu.make_async_remote_copy(
            src_ref=bins.at[0, rows, :], dst_ref=level_bins.at[level],
            send_sem=bins_send.at[sem], recv_sem=bins_recv.at[level],
            device_id={"depth": target}, device_id_type=MESH,
        )

    def send_bins(step, carry):
        bins_copy((here + step) % depth, here, step).start()
        return carry

    lax.fori_loop(1, depth, send_bins, 0)

    up = group * strips + snake(jnp.maximum(strip - 1, 0))
    down = group * strips + snake(jnp.minimum(strip + 1, strips - 1))

    def halo_copy(slot, f, way):
        source = HALO if way == 0 else ROWS
        target = HALO + ROWS if way == 0 else 0
        return pltpu.make_async_remote_copy(
            src_ref=field.at[slot, f, :, pl.ds(source, HALO), :],
            dst_ref=field.at[slot, f, :, pl.ds(target, HALO), :],
            send_sem=halo_send.at[way, slot, f], recv_sem=halo_recv.at[way, slot, f],
            device_id={"depth": up if way == 0 else down}, device_id_type=MESH,
        )

    def swap_copy(index):
        return pltpu.make_async_remote_copy(
            src_ref=part.at[index, pl.ds((1 - core) * share, share)], dst_ref=mirror.at[index],
            send_sem=swap_send.at[index], recv_sem=swap_recv.at[index],
            device_id={"freq": 1 - core}, device_id_type=MESH,
        )

    out_core = strip // per_core

    def out_copy(index, from_core, from_place):
        rows = pl.ds(pl.multiple_of(from_place * ROWS, ROWS), ROWS)
        return pltpu.make_async_remote_copy(
            src_ref=total.at[index], dst_ref=out.at[pl.ds(from_core * share, share), rows, :],
            send_sem=out_send.at[index], recv_sem=out_recv.at[from_core, from_place],
            device_id={"depth": group * strips + index, "freq": out_core}, device_id_type=MESH,
        )

    def owned(index):
        return (group * strips + index == here) & (out_core == core)

    def deliver(index):
        swap_copy(index).wait()
        mine = part[index, pl.ds(core * share, share)] + mirror[index]

        @pl.when(owned(index))
        def _():
            rows = pl.ds(pl.multiple_of(strip % per_core * ROWS, ROWS), ROWS)
            out[pl.ds(core * share, share), rows, :] = mine

        @pl.when(jnp.logical_not(owned(index)))
        def _():
            total[index] = mine
            out_copy(index, core, strip % per_core).start()

    wide = lax.broadcasted_iota(jnp.int32, (WINDOW, width), 1)
    lane = lax.broadcasted_iota(jnp.int32, (ROWS, width), 1)

    def level(z, carry):
        slot = z % 2
        after = 1 - slot

        for f in range(freq_count):
            for way, has_send, has_recv in ((0, has_up, has_down), (1, has_down, has_up)):

                @pl.when((z > 0) & has_recv)
                def _():
                    halo_copy(slot, f, way).wait_recv()

                @pl.when((z > 0) & has_send)
                def _():
                    halo_copy(slot, f, way).wait_send()

            for j in range(PARTS):
                values = field[slot, f, j]
                cols = slice(j * width, (j + 1) * width)
                for b in range(TAPS):
                    reach = b - HALF
                    moved = values
                    if reach:
                        moved = pltpu.roll(values, (-reach) % width, 1)
                        inside = wide < width - reach if reach > 0 else wide >= -reach
                        moved = jnp.where(inside, moved, 0.0)
                    high, low = split(moved)
                    if b < TAPS - 1:
                        places = [b * WINDOW + n * MAIN for n in range(3)]
                    else:
                        places = [3 * MAIN + n * WINDOW for n in range(3)]
                    for place, piece in zip(places, (high, low, high)):
                        patches[f, place : place + WINDOW, cols] = piece
            result = jnp.dot(taps[f], patches[f], preferred_element_type=jnp.float32)

            if f == 0:

                @pl.when(z != here)
                def _():
                    bins_copy(here, z, 0).wait_recv()

            chosen = level_bins[z]
            picked = None
            for k in range(kernels):
                rows = [
                    [
                        result[
                            (2 * k + c) * ROWS : (2 * k + c + 1) * ROWS,
                            j * width : (j + 1) * width,
                        ]
                        for j in range(PARTS)
                    ]
                    for c in range(2)
                ]
                if picked is None:
                    picked = rows
                else:
                    mask = chosen == k
                    picked = [
                        [jnp.where(mask, rows[c][j], picked[c][j]) for j in range(PARTS)]
                        for c in range(2)
                    ]
            for pair in range(PARTS // 2):
                re, im = 2 * pair, 2 * pair + 1
                field[after, f, re, pl.ds(HALO, ROWS), :] = picked[0][re] - picked[1][im]
                field[after, f, im, pl.ds(HALO, ROWS), :] = picked[0][im] + picked[1][re]

            for way, has_send in ((0, has_up), (1, has_down)):

                @pl.when((z < depth - 1) & has_send)
                def _():
                    halo_copy(after, f, way).start()

        index = z - group * strips

        @pl.when((index >= 0) & (index < strips))
        def _():
            for n in range(lag_count):
                lag = lags[n]
                back = lax.rem(width - 2 * lag, width)
                product = jnp.zeros((ROWS, width), jnp.float32)
                for f in range(freq_count):
                    for j in range(PARTS // 2):
                        source = field[after, f, j, pl.ds(HALO, ROWS), :]
                        receiver = field[after, f, 2 + j, pl.ds(HALO, ROWS), :]
                        product += source * pltpu.roll(receiver, back, 1)
                product = jnp.where(lane < width - 2 * lag, product, 0.0)
                part[index, n] = pltpu.roll(product, lag, 1)
            swap_copy(index).start()

        @pl.when((index >= 1) & (index <= strips))
        def _():
            deliver(index - 1)

        return carry

    lax.fori_loop(0, depth, level, 0)

    @pl.when(group == groups - 1)
    def _():
        deliver(strips - 1)

    def finish_out(index, carry):
        @pl.when(jnp.logical_not(owned(index)))
        def _():
            out_copy(index, core, strip % per_core).wait_send()

        return carry

    def finish_bins(step, carry):
        bins_copy((here + step) % depth, here, step).wait_send()
        return carry

    for from_core in range(freqs):
        for place in range(per_core):
            sender = core * per_core + place

            @pl.when((sender != strip) | (core != from_core))
            def _():
                out_copy(0, from_core, place).wait_recv()

    lax.fori_loop(0, strips, finish_out, 0)
    lax.fori_loop(1, depth, finish_bins, 0)


def body(surface, bins, stencil, phase_step, phase_shift, lags, *, depth, freqs):
    freq_count = surface.shape[1]
    height = surface.shape[3]
    width = surface.shape[4] // 2
    kernels = stencil.shape[1]
    lag_count = lags.shape[0]
    strips = height // ROWS
    groups = depth // strips
    per_core = strips // freqs
    share = lag_count // freqs
    tiles = -(-TAPS // PER_TILE)
    cost = 2 * freq_count * depth * 2 * kernels * ROWS * CONTRACT * PARTS * width
    vmem = pl.BlockSpec(memory_space=pltpu.VMEM)
    image = pl.pallas_call(
        functools.partial(kernel, depth, groups, freqs),
        out_shape=jax.ShapeDtypeStruct((lag_count, per_core * ROWS, width), jnp.float32),
        in_specs=[vmem] * 5 + [pl.BlockSpec(memory_space=pltpu.SMEM)],
        out_specs=vmem,
        scratch_shapes=[
            pltpu.VMEM((2, freq_count, PARTS, WINDOW, width), jnp.float32),
            pltpu.VMEM((depth, ROWS, width), jnp.int32),
            pltpu.VMEM((freq_count, tiles, 2 * kernels * ROWS, LANES), jnp.float32),
            pltpu.VMEM((freq_count, 2 * kernels * ROWS, CONTRACT), jnp.bfloat16),
            pltpu.VMEM((freq_count, CONTRACT, PARTS * width), jnp.bfloat16),
            pltpu.VMEM((strips, lag_count, ROWS, width), jnp.float32),
            pltpu.VMEM((strips, share, ROWS, width), jnp.float32),
            pltpu.VMEM((strips, share, ROWS, width), jnp.float32),
            pltpu.SemaphoreType.DMA((depth,)),
            pltpu.SemaphoreType.DMA((depth,)),
            pltpu.SemaphoreType.DMA((2, 2, freq_count)),
            pltpu.SemaphoreType.DMA((2, 2, freq_count)),
            pltpu.SemaphoreType.DMA((strips,)),
            pltpu.SemaphoreType.DMA((strips,)),
            pltpu.SemaphoreType.DMA((strips,)),
            pltpu.SemaphoreType.DMA((freqs, per_core)),
        ],
        compiler_params=pltpu.CompilerParams(
            collective_id=0, has_side_effects=True, vmem_limit_bytes=32 * 1024 * 1024
        ),
        cost_estimate=pl.CostEstimate(flops=cost, bytes_accessed=1 << 20, transcendentals=0),
    )(surface, bins, stencil, phase_step, phase_shift, lags)
    return image.reshape(1, lag_count, per_core * ROWS * width)


def solution(mesh):
    return jax.shard_map(
        functools.partial(body, depth=mesh.shape["depth"], freqs=mesh.shape["freq"]),
        mesh=mesh,
        in_specs=(
            P("shots", "freq", None, None, None),
            P("depth", None, None),
            P("freq", None, None),
            P("freq", None),
            P("freq", None),
            P(),
        ),
        out_specs=P("depth", "shots", "freq"),
        check_vma=False,
    )
```

time: 385 us -> 42.9 us (0.11)
  waiting for transfers between devices: 154 us -> 0 us
  starting transfers between devices: 115 us -> 0 us
  local copies, waits for them, and re-layouts: 56.1 us -> 3.4 us
  Pallas kernels: 0 us -> 39.2 us
  loops' own time: 21.4 us -> 0 us
  matrix products: 18.3 us -> 0 us
  between operations: 13.5 us -> 0.02 us
  other arithmetic: 5.48 us -> 0 us
    unnamed x2 -> x0, waiting for transfers between devices: 116 us -> none
    ppermute x9 -> x0, starting transfers between devices: 115 us -> none  [from_behind(): lax.ppermute(value, axis, [(source, source + steps) for source in range(i...]
    pallas_call x0 -> x1, Pallas kernels: none -> 39.2 us  [body(): pl.pallas_call(functools.partial(kernel, depth, groups, freqs), out_shape...]
    ppermute x9 -> x0, waiting for transfers between devices: 38.1 us -> none  [from_behind(): lax.ppermute(value, axis, [(source, source + steps) for source in range(i...]
    another operation x10 -> x0, loops' own time: 21.4 us -> none  [the longest x9 20.5 us: advance_turn(): return lax.cond(active, compute_front, keep_state, (incoming, image_now))]
    dot_general x3 -> x0, matrix products: 18.3 us -> none  [the longest x2 12.6 us: advance_level(): jnp.dot(patches, weights, precision=lax.Precision.HIGHEST, preferred_elem...]
    unnamed x9 -> x11, local copies, waits for them, and re-layouts: 16.4 us -> 2.7 us
    another operation x4 -> x0, local copies, waits for them, and re-layouts: 11.8 us -> none  [advance_level(): jnp.stack([windows[:, row_tap:row_tap + grid_width] for row_tap in range(...]
  transfers between devices with their start and end apart: 10 -> 0, of which waited for: 10 -> 0; matrix products, arithmetic and copies ran while one was open for 0% -> 0% of each run, Pallas kernels for 0% -> 0%
where the time goes in v1:
time: 42.9 us; the launch traced here: 42.6 us
  Pallas kernels  39.2 us (91%)
  local copies, waits for them, and re-layouts  3.4 us (8%)
    pallas_call x1, Pallas kernels, body(): pl.pallas_call(functools.partial(kernel, depth, groups, freqs), out_shape...  39.2 us
    unnamed x11, local copies, waits for them, and re-layouts  2.7 us

profile of v1, /device:TPU:0, one launch (start us, length us, event | category | flops | bytes accessed | tf_op | source)
XLA Modules:
  0.0 42.6 jit_solution(5420902281302090558)
XLA Ops:
  0.0 0.0 copy-start.4
  0.0 0.0 copy-start.3
  0.0 0.0 copy-start.2
  0.0 0.8 %copy.7.stencil = f32[2,8,5]{2,1,0:T(8,128)S(1)} copy(f32[2,8,5]{1,0,2:T(2,128)} %param.8) | data formatting | bytes 640 | tf_op args[2]
  0.8 0.0 copy-done.4
  0.8 0.0 copy-done.3
  0.8 0.0 copy-done.2
  0.8 0.0 copy-start
  0.8 1.0 %copy-done = f32[1,2,2,128,256]{4,3,2,1,0:T(8,128)S(1)} copy-done((f32[1,2,2,128,256]{4,3,2,1,0:T(8,128)S(1)}, f32[1,2,2,128,256]{4,3,2,1,0:T(8,128)}, u32[]{:S(2)}) %copy-start) | copy-done | bytes 524312
  1.9 0.0 copy-start.1
  1.9 0.8 %copy-done.1 = s32[1,128,128]{2,1,0:T(8,128)S(1)} copy-done((s32[1,128,128]{2,1,0:T(8,128)S(1)}, s32[1,128,128]{2,1,0:T(8,128)}, u32[]{:S(2)}) %copy-start.1) | copy-done | bytes 65560
  2.7 39.2 %shard_map.64 = f32[4,64,128]{2,1,0:T(8,128)S(1)} custom-call(f32[1,2,2,128,256]{4,3,2,1,0:T(8,128)S(1)} %copy-done, s32[1,128,128]{2,1,0:T(8,128)S(1)} %copy-done.1, f32[2,8,5]{2,1,0:T(8,128)S(1)} %copy.7.stencil, f32[2,8]{1,0:T(2,128)S(1)} %copy-done.2, f32[2,8]{1,0:T(2,128)S(1)} %copy-done.3, s32[4]{0:T(128)S(1)} %copy-done.4), custom_call_target="tpu_custom_call" | custom-call | flops 5368709120 | bytes 1048576 | tf_op jit(solution)/shard_map/pallas_call | solution.py:359
  41.9 0.7 %reshape.3 = f32[1,4,8192]{2,1,0:T(4,128)} reshape(f32[4,64,128]{2,1,0:T(8,128)S(1)} %shard_map.64) | data formatting | bytes 262144 | tf_op jit(solution)/shard_map/reshape | solution.py:387
Async XLA Ops:
  0.0 0.8 %copy-start.4 = (s32[4]{0:T(128)S(1)}, s32[4]{0:T(128)}, u32[]{:S(2)}) copy-start(s32[4]{0:T(128)} %lags.1) | copy-start | bytes 52
  0.0 0.8 %copy-start.3 = (f32[2,8]{1,0:T(2,128)S(1)}, f32[2,8]{1,0:T(2,128)}, u32[]{:S(2)}) copy-start(f32[2,8]{1,0:T(2,128)} %phase_shift.1) | copy-start | bytes 196
  0.0 0.8 %copy-start.2 = (f32[2,8]{1,0:T(2,128)S(1)}, f32[2,8]{1,0:T(2,128)}, u32[]{:S(2)}) copy-start(f32[2,8]{1,0:T(2,128)} %phase_step.1) | copy-start | bytes 196
  0.8 1.0 %copy-start = (f32[1,2,2,128,256]{4,3,2,1,0:T(8,128)S(1)}, f32[1,2,2,128,256]{4,3,2,1,0:T(8,128)}, u32[]{:S(2)}) copy-start(f32[1,2,2,128,256]{4,3,2,1,0:T(8,128)} %surface.1) | copy-start | bytes 1572868
  1.9 0.8 %copy-start.1 = (s32[1,128,128]{2,1,0:T(8,128)S(1)}, s32[1,128,128]{2,1,0:T(8,128)}, u32[]{:S(2)}) copy-start(s32[1,128,128]{2,1,0:T(8,128)} %bins.1) | copy-start | bytes 196612

commit v2 on v1

--- a/solution.py
+++ b/solution.py
@@ -34,7 +34,7 @@
 
 
 def build_taps(weights, step, shift, kernels):
-    center, along_x, along_y, main, anti = (weights[:, j : j + 1] for j in range(5))
+    center, along_x, along_y, main, anti = weights
     scale = step / (center + 2.0 * (along_x + along_y + main + anti))
     center, along_x, along_y, main, anti = (
         jnp.broadcast_to(part * scale, (kernels, LANES))
@@ -85,10 +85,10 @@
     depth, groups, freqs,
     surface, bins, stencil, phase_step, phase_shift, lags, out,
     field, level_bins, spread, taps, patches, part, mirror, total,
-    bins_send, bins_recv, halo_send, halo_recv, swap_send, swap_recv, out_send, out_recv,
+    load_sem, bins_send, bins_recv, halo_send, halo_recv, swap_send, swap_recv, out_send, out_recv,
 ):
     freq_count = surface.shape[1]
-    kernels = stencil.shape[1]
+    kernels = stencil.shape[2]
     width = surface.shape[4] // 2
     lag_count = lags.shape[0]
     strips = depth // groups
@@ -103,22 +103,23 @@
 
     field[...] = jnp.zeros_like(field)
     first = pl.multiple_of(strip * ROWS, ROWS)
-    for f in range(freq_count):
-        for j in range(PARTS):
-            cols = pl.ds((j % 2) * width, width)
-            field[0, f, j, pl.ds(HALO, ROWS), :] = surface[0, f, j // 2, pl.ds(first, ROWS), cols]
-
-            @pl.when(has_up)
-            def _():
-                above = pl.multiple_of(jnp.maximum(first - HALO, 0), HALO)
-                field[0, f, j, pl.ds(0, HALO), :] = surface[0, f, j // 2, pl.ds(above, HALO), cols]
-
-            @pl.when(has_down)
-            def _():
-                below = pl.multiple_of(jnp.minimum(first + ROWS, (strips - 1) * ROWS), HALO)
-                field[0, f, j, pl.ds(HALO + ROWS, HALO), :] = surface[
-                    0, f, j // 2, pl.ds(below, HALO), cols
-                ]
+
+    def load_copy(c, place):
+        rows = (first, jnp.maximum(first - HALO, 0), jnp.minimum(first + ROWS, strips * ROWS - HALO))
+        size = (ROWS, HALO, HALO)[place]
+        target = (HALO, 0, HALO + ROWS)[place]
+        return pltpu.make_async_copy(
+            surface.at[0, :, :, pl.ds(pl.multiple_of(rows[place], HALO), size), pl.ds(c * width, width)],
+            field.at[0, :, :, c, pl.ds(target, size), :],
+            load_sem.at[c, place],
+        )
+
+    own_bins = pltpu.make_async_copy(bins.at[0, pl.ds(first, ROWS), :], level_bins.at[here], bins_send.at[0])
+    own_bins.start()
+    for c in range(2):
+        load_copy(c, 0).start()
+        pl.when(has_up)(load_copy(c, 1).start)
+        pl.when(has_down)(load_copy(c, 2).start)
 
     barrier = pltpu.get_barrier_semaphore()
 
@@ -132,12 +133,12 @@
 
     lax.fori_loop(1, depth * freqs, greet, 0)
 
-    level_bins[here] = bins[0, pl.ds(first, ROWS), :]
     for f in range(freq_count):
         patches[f, 3 * MAIN + 3 * WINDOW :, :] = jnp.zeros((WINDOW, PARTS * width), jnp.bfloat16)
         step = column(phase_step[f : f + 1, :], kernels)
         shift = column(phase_shift[f : f + 1, :], kernels)
-        kern = build_taps(stencil[f], step, shift, kernels)
+        weights = [column(stencil[j, f : f + 1, :], kernels) for j in range(5)]
+        kern = build_taps(weights, step, shift, kernels)
         for c in range(2):
             for t in range(len(kern[c])):
                 for y in range(ROWS):
@@ -153,6 +154,11 @@
         last = high + pltpu.roll(high, WINDOW, 1) + pltpu.roll(low, 2 * WINDOW, 1)
         taps[f, :, 3 * MAIN :] = last.astype(jnp.bfloat16)
 
+    own_bins.wait()
+    for c in range(2):
+        load_copy(c, 0).wait()
+        pl.when(has_up)(load_copy(c, 1).wait)
+        pl.when(has_down)(load_copy(c, 2).wait)
     pl.semaphore_wait(barrier, depth * freqs - 1)
 
     def bins_copy(target, level, sem):
@@ -176,8 +182,8 @@
         source = HALO if way == 0 else ROWS
         target = HALO + ROWS if way == 0 else 0
         return pltpu.make_async_remote_copy(
-            src_ref=field.at[slot, f, :, pl.ds(source, HALO), :],
-            dst_ref=field.at[slot, f, :, pl.ds(target, HALO), :],
+            src_ref=field.at[slot, f, :, :, pl.ds(source, HALO), :],
+            dst_ref=field.at[slot, f, :, :, pl.ds(target, HALO), :],
             send_sem=halo_send.at[way, slot, f], recv_sem=halo_recv.at[way, slot, f],
             device_id={"depth": up if way == 0 else down}, device_id_type=MESH,
         )
@@ -202,19 +208,24 @@
     def owned(index):
         return (group * strips + index == here) & (out_core == core)
 
+    def collect(index):
+        swap_copy(index).wait()
+        total[index] = part[index, pl.ds(core * share, share)] + mirror[index]
+
     def deliver(index):
-        swap_copy(index).wait()
-        mine = part[index, pl.ds(core * share, share)] + mirror[index]
-
         @pl.when(owned(index))
         def _():
             rows = pl.ds(pl.multiple_of(strip % per_core * ROWS, ROWS), ROWS)
-            out[pl.ds(core * share, share), rows, :] = mine
+            out[pl.ds(core * share, share), rows, :] = total[index]
 
         @pl.when(jnp.logical_not(owned(index)))
         def _():
-            total[index] = mine
             out_copy(index, core, strip % per_core).start()
+
+    def deliver_early(step, carry):
+        index = (strip + step) % strips
+        pl.when(index < strips - 1)(lambda: deliver(index))
+        return carry
 
     wide = lax.broadcasted_iota(jnp.int32, (WINDOW, width), 1)
     lane = lax.broadcasted_iota(jnp.int32, (ROWS, width), 1)
@@ -222,6 +233,7 @@
     def level(z, carry):
         slot = z % 2
         after = 1 - slot
+        index = z - group * strips
 
         for f in range(freq_count):
             for way, has_send, has_recv in ((0, has_up, has_down), (1, has_down, has_up)):
@@ -234,8 +246,17 @@
                 def _():
                     halo_copy(slot, f, way).wait_send()
 
+            if f == freq_count - 1:
+                pl.when((index >= 1) & (index <= strips))(lambda: collect(index - 1))
+
+                @pl.when(index == strips - 1)
+                def _():
+                    lax.fori_loop(1, strips + 1, deliver_early, 0)
+
+                pl.when(index == strips)(lambda: deliver(strips - 1))
+
             for j in range(PARTS):
-                values = field[slot, f, j]
+                values = field[slot, f, j // 2, j % 2]
                 cols = slice(j * width, (j + 1) * width)
                 for b in range(TAPS):
                     reach = b - HALF
@@ -282,16 +303,14 @@
                     ]
             for pair in range(PARTS // 2):
                 re, im = 2 * pair, 2 * pair + 1
-                field[after, f, re, pl.ds(HALO, ROWS), :] = picked[0][re] - picked[1][im]
-                field[after, f, im, pl.ds(HALO, ROWS), :] = picked[0][im] + picked[1][re]
+                field[after, f, pair, 0, pl.ds(HALO, ROWS), :] = picked[0][re] - picked[1][im]
+                field[after, f, pair, 1, pl.ds(HALO, ROWS), :] = picked[0][im] + picked[1][re]
 
             for way, has_send in ((0, has_up), (1, has_down)):
 
                 @pl.when((z < depth - 1) & has_send)
                 def _():
                     halo_copy(after, f, way).start()
-
-        index = z - group * strips
 
         @pl.when((index >= 0) & (index < strips))
         def _():
@@ -301,23 +320,20 @@
                 product = jnp.zeros((ROWS, width), jnp.float32)
                 for f in range(freq_count):
                     for j in range(PARTS // 2):
-                        source = field[after, f, j, pl.ds(HALO, ROWS), :]
-                        receiver = field[after, f, 2 + j, pl.ds(HALO, ROWS), :]
+                        source = field[after, f, 0, j, pl.ds(HALO, ROWS), :]
+                        receiver = field[after, f, 1, j, pl.ds(HALO, ROWS), :]
                         product += source * pltpu.roll(receiver, back, 1)
                 product = jnp.where(lane < width - 2 * lag, product, 0.0)
                 part[index, n] = pltpu.roll(product, lag, 1)
             swap_copy(index).start()
 
-        @pl.when((index >= 1) & (index <= strips))
-        def _():
-            deliver(index - 1)
-
         return carry
 
     lax.fori_loop(0, depth, level, 0)
 
     @pl.when(group == groups - 1)
     def _():
+        collect(strips - 1)
         deliver(strips - 1)
 
     def finish_out(index, carry):
@@ -359,10 +375,10 @@
     image = pl.pallas_call(
         functools.partial(kernel, depth, groups, freqs),
         out_shape=jax.ShapeDtypeStruct((lag_count, per_core * ROWS, width), jnp.float32),
-        in_specs=[vmem] * 5 + [pl.BlockSpec(memory_space=pltpu.SMEM)],
+        in_specs=[pl.BlockSpec(memory_space=pl.ANY)] * 2 + [vmem] * 3 + [pl.BlockSpec(memory_space=pltpu.SMEM)],
         out_specs=vmem,
         scratch_shapes=[
-            pltpu.VMEM((2, freq_count, PARTS, WINDOW, width), jnp.float32),
+            pltpu.VMEM((2, freq_count, PARTS // 2, 2, WINDOW, width), jnp.float32),
             pltpu.VMEM((depth, ROWS, width), jnp.int32),
             pltpu.VMEM((freq_count, tiles, 2 * kernels * ROWS, LANES), jnp.float32),
             pltpu.VMEM((freq_count, 2 * kernels * ROWS, CONTRACT), jnp.bfloat16),
@@ -370,6 +386,7 @@
             pltpu.VMEM((strips, lag_count, ROWS, width), jnp.float32),
             pltpu.VMEM((strips, share, ROWS, width), jnp.float32),
             pltpu.VMEM((strips, share, ROWS, width), jnp.float32),
+            pltpu.SemaphoreType.DMA((2, 3)),
             pltpu.SemaphoreType.DMA((depth,)),
             pltpu.SemaphoreType.DMA((depth,)),
             pltpu.SemaphoreType.DMA((2, 2, freq_count)),
@@ -383,7 +400,7 @@
             collective_id=0, has_side_effects=True, vmem_limit_bytes=32 * 1024 * 1024
         ),
         cost_estimate=pl.CostEstimate(flops=cost, bytes_accessed=1 << 20, transcendentals=0),
-    )(surface, bins, stencil, phase_step, phase_shift, lags)
+    )(surface, bins, jnp.transpose(stencil, (2, 0, 1)), phase_step, phase_shift, lags)
     return image.reshape(1, lag_count, per_core * ROWS * width)
 
 

time: 42.9 us -> 45.2 us (1.054); the launches traced: 42.6 us -> 44.4 us
  local copies, waits for them, and re-layouts: 3.4 us -> 4.65 us
  Pallas kernels: 39.2 us -> 39.7 us
    unnamed x11 -> x12, local copies, waits for them, and re-layouts: 2.7 us -> 3.94 us
    pallas_call x1, Pallas kernels: 39.2 us -> 39.7 us  [body(): pl.pallas_call(functools.partial(kernel, depth, groups, freqs), out_shape...]
where the time goes in v2:
time: 45.2 us; the launch traced here: 44.4 us
  Pallas kernels  39.7 us (88%)
  local copies, waits for them, and re-layouts  4.65 us (10%)
    pallas_call x1, Pallas kernels, body(): pl.pallas_call(functools.partial(kernel, depth, groups, freqs), out_shape...  39.7 us
    unnamed x12, local copies, waits for them, and re-layouts  3.94 us

profile of v2, /device:TPU:0, one launch (start us, length us, event | category | flops | bytes accessed | tf_op | source)
XLA Modules:
  0.0 44.4 jit_solution(1477019058580183611)
XLA Ops:
  0.0 0.0 copy-start.5
  0.0 0.0 copy-start.3
  0.0 0.7 %copy-done.5 = s32[4]{0:T(128)S(1)} copy-done((s32[4]{0:T(128)S(1)}, s32[4]{0:T(128)}, u32[]{:S(2)}) %copy-start.5) | copy-done | bytes 40
  0.7 0.0 copy-done.3
  0.7 0.0 copy-start
  0.7 1.0 %copy-done = f32[1,2,2,128,256]{4,3,2,1,0:T(8,128)S(1)} copy-done((f32[1,2,2,128,256]{4,3,2,1,0:T(8,128)S(1)}, f32[1,2,2,128,256]{4,3,2,1,0:T(8,128)}, u32[]{:S(2)}) %copy-start) | copy-done | bytes 524312
  1.7 0.0 copy-start.1
  1.7 0.8 %copy-done.1 = s32[1,128,128]{2,1,0:T(8,128)S(1)} copy-done((s32[1,128,128]{2,1,0:T(8,128)S(1)}, s32[1,128,128]{2,1,0:T(8,128)}, u32[]{:S(2)}) %copy-start.1) | copy-done | bytes 65560
  2.6 0.0 copy-start.2
  2.6 0.7 %copy-done.2 = f32[2,8,5]{1,0,2:T(2,128)S(1)} copy-done((f32[2,8,5]{1,0,2:T(2,128)S(1)}, f32[2,8,5]{1,0,2:T(2,128)}, u32[]{:S(2)}) %copy-start.2) | copy-done | bytes 344
  3.3 0.0 copy-start.4
  3.3 0.7 %copy-done.4 = f32[2,8]{1,0:T(2,128)S(1)} copy-done((f32[2,8]{1,0:T(2,128)S(1)}, f32[2,8]{1,0:T(2,128)}, u32[]{:S(2)}) %copy-start.4) | copy-done | bytes 88
  3.9 39.7 %shard_map.64 = f32[4,64,128]{2,1,0:T(8,128)S(1)} custom-call(f32[1,2,2,128,256]{4,3,2,1,0:T(8,128)S(1)} %copy-done, s32[1,128,128]{2,1,0:T(8,128)S(1)} %copy-done.1, f32[5,2,8]{2,1,0:T(2,128)S(1)} %bitcast.1, f32[2,8]{1,0:T(2,128)S(1)} %copy-done.3, f32[2,8]{1,0:T(2,128)S(1)} %copy-done.4, s32[4]{0:T(128)S(1)} %copy-done.5), custom_call_target="tpu_custom_call" | custom-call | flops 5368709120 | bytes 1048576 | tf_op jit(solution)/shard_map/pallas_call | solution.py:375
  43.7 0.7 %reshape.3 = f32[1,4,8192]{2,1,0:T(4,128)} reshape(f32[4,64,128]{2,1,0:T(8,128)S(1)} %shard_map.64) | data formatting | bytes 262144 | tf_op jit(solution)/shard_map/reshape | solution.py:404
Async XLA Ops:
  0.0 0.7 %copy-start.5 = (s32[4]{0:T(128)S(1)}, s32[4]{0:T(128)}, u32[]{:S(2)}) copy-start(s32[4]{0:T(128)} %lags.1) | copy-start | bytes 52
  0.0 0.7 %copy-start.3 = (f32[2,8]{1,0:T(2,128)S(1)}, f32[2,8]{1,0:T(2,128)}, u32[]{:S(2)}) copy-start(f32[2,8]{1,0:T(2,128)} %phase_step.1) | copy-start | bytes 196
  0.7 1.0 %copy-start = (f32[1,2,2,128,256]{4,3,2,1,0:T(8,128)S(1)}, f32[1,2,2,128,256]{4,3,2,1,0:T(8,128)}, u32[]{:S(2)}) copy-start(f32[1,2,2,128,256]{4,3,2,1,0:T(8,128)} %surface.1) | copy-start | bytes 1572868
  1.7 0.8 %copy-start.1 = (s32[1,128,128]{2,1,0:T(8,128)S(1)}, s32[1,128,128]{2,1,0:T(8,128)}, u32[]{:S(2)}) copy-start(s32[1,128,128]{2,1,0:T(8,128)} %bins.1) | copy-start | bytes 196612
  2.6 0.7 %copy-start.2 = (f32[2,8,5]{1,0,2:T(2,128)S(1)}, f32[2,8,5]{1,0,2:T(2,128)}, u32[]{:S(2)}) copy-start(f32[2,8,5]{1,0,2:T(2,128)} %param.8) | copy-start | bytes 964
  3.3 0.7 %copy-start.4 = (f32[2,8]{1,0:T(2,128)S(1)}, f32[2,8]{1,0:T(2,128)}, u32[]{:S(2)}) copy-start(f32[2,8]{1,0:T(2,128)} %phase_shift.1) | copy-start | bytes 196

commit v3 on v2

--- a/solution.py
+++ b/solution.py
@@ -83,7 +83,8 @@
 
 def kernel(
     depth, groups, freqs,
-    surface, bins, stencil, phase_step, phase_shift, lags, out,
+    surface, bins, stencil_far, phase_step_far, phase_shift_far, lags_far, out,
+    stencil, phase_step, phase_shift, lags, small_sem,
     field, level_bins, spread, taps, patches, part, mirror, total,
     load_sem, bins_send, bins_recv, halo_send, halo_recv, swap_send, swap_recv, out_send, out_recv,
 ):
@@ -114,6 +115,15 @@
             load_sem.at[c, place],
         )
 
+    smalls = [
+        pltpu.make_async_copy(far, near, small_sem.at[n])
+        for n, (far, near) in enumerate((
+            (stencil_far, stencil), (phase_step_far, phase_step),
+            (phase_shift_far, phase_shift), (lags_far, lags),
+        ))
+    ]
+    for small in smalls:
+        small.start()
     own_bins = pltpu.make_async_copy(bins.at[0, pl.ds(first, ROWS), :], level_bins.at[here], bins_send.at[0])
     own_bins.start()
     for c in range(2):
@@ -133,6 +143,8 @@
 
     lax.fori_loop(1, depth * freqs, greet, 0)
 
+    for small in smalls:
+        small.wait()
     for f in range(freq_count):
         patches[f, 3 * MAIN + 3 * WINDOW :, :] = jnp.zeros((WINDOW, PARTS * width), jnp.bfloat16)
         step = column(phase_step[f : f + 1, :], kernels)
@@ -256,16 +268,17 @@
                 pl.when(index == strips)(lambda: deliver(strips - 1))
 
             for j in range(PARTS):
-                values = field[slot, f, j // 2, j % 2]
+                halves = split(field[slot, f, j // 2, j % 2])
                 cols = slice(j * width, (j + 1) * width)
                 for b in range(TAPS):
                     reach = b - HALF
-                    moved = values
+                    high, low = halves
                     if reach:
-                        moved = pltpu.roll(values, (-reach) % width, 1)
                         inside = wide < width - reach if reach > 0 else wide >= -reach
-                        moved = jnp.where(inside, moved, 0.0)
-                    high, low = split(moved)
+                        high, low = (
+                            jnp.where(inside, pltpu.roll(half, (-reach) % width, 1), jnp.zeros_like(half))
+                            for half in halves
+                        )
                     if b < TAPS - 1:
                         places = [b * WINDOW + n * MAIN for n in range(3)]
                     else:
@@ -375,9 +388,14 @@
     image = pl.pallas_call(
         functools.partial(kernel, depth, groups, freqs),
         out_shape=jax.ShapeDtypeStruct((lag_count, per_core * ROWS, width), jnp.float32),
-        in_specs=[pl.BlockSpec(memory_space=pl.ANY)] * 2 + [vmem] * 3 + [pl.BlockSpec(memory_space=pltpu.SMEM)],
+        in_specs=[pl.BlockSpec(memory_space=pl.ANY)] * 6,
         out_specs=vmem,
         scratch_shapes=[
+            pltpu.VMEM((stencil.shape[2], freq_count, kernels), jnp.float32),
+            pltpu.VMEM(phase_step.shape, jnp.float32),
+            pltpu.VMEM(phase_shift.shape, jnp.float32),
+            pltpu.SMEM(lags.shape, jnp.int32),
+            pltpu.SemaphoreType.DMA((4,)),
             pltpu.VMEM((2, freq_count, PARTS // 2, 2, WINDOW, width), jnp.float32),
             pltpu.VMEM((depth, ROWS, width), jnp.int32),
             pltpu.VMEM((freq_count, tiles, 2 * kernels * ROWS, LANES), jnp.float32),
@@ -397,7 +415,7 @@
             pltpu.SemaphoreType.DMA((freqs, per_core)),
         ],
         compiler_params=pltpu.CompilerParams(
-            collective_id=0, has_side_effects=True, vmem_limit_bytes=32 * 1024 * 1024
+            collective_id=0, has_side_effects=True, vmem_limit_bytes=60 * 1024 * 1024
         ),
         cost_estimate=pl.CostEstimate(flops=cost, bytes_accessed=1 << 20, transcendentals=0),
     )(surface, bins, jnp.transpose(stencil, (2, 0, 1)), phase_step, phase_shift, lags)

time: 45.2 us -> 41.4 us (0.916)
  local copies, waits for them, and re-layouts: 4.65 us -> 1.61 us
    unnamed x12 -> x0, local copies, waits for them, and re-layouts: 3.94 us -> none
    reshape x1, local copies, waits for them, and re-layouts: 0.71 us -> 1.61 us  [body(): return image.reshape(1, lag_count, per_core * ROWS * width)]
where the time goes in v3:
time: 41.4 us; the launch traced here: 41 us
  Pallas kernels  39.4 us (95%)
  local copies, waits for them, and re-layouts  1.61 us (4%)
    pallas_call x1, Pallas kernels, body(): pl.pallas_call(functools.partial(kernel, depth, groups, freqs), out_shape...  39.4 us
    reshape x1, local copies, waits for them, and re-layouts, body(): return image.reshape(1, lag_count, per_core * ROWS * width)  1.61 us

profile of v3, /device:TPU:0, one launch (start us, length us, event | category | flops | bytes accessed | tf_op | source)
XLA Modules:
  0.0 41.0 jit_solution(4136359064019028394)
XLA Ops:
  0.0 39.4 %shard_map.64 = f32[4,64,128]{2,1,0:T(8,128)} custom-call(f32[1,2,2,128,256]{4,3,2,1,0:T(8,128)} %surface.1, s32[1,128,128]{2,1,0:T(8,128)} %bins.1, f32[5,2,8]{2,1,0:T(2,128)} %bitcast.1, f32[2,8]{1,0:T(2,128)} %phase_step_far.1, f32[2,8]{1,0:T(2,128)} %phase_shift_far.1, s32[4]{0:T(128)} %lags_far.1), custom_call_target="tpu_custom_call" | custom-call | flops 5368709120 | bytes 1048576 | tf_op jit(solution)/shard_map/pallas_call | solution.py:388
  39.4 1.6 %reshape.3 = f32[1,4,8192]{2,1,0:T(4,128)} reshape(f32[4,64,128]{2,1,0:T(8,128)} %shard_map.64) | data formatting | bytes 262144 | tf_op jit(solution)/shard_map/reshape | solution.py:422

commit v4 on v3

--- a/solution.py
+++ b/solution.py
@@ -85,7 +85,7 @@
     depth, groups, freqs,
     surface, bins, stencil_far, phase_step_far, phase_shift_far, lags_far, out,
     stencil, phase_step, phase_shift, lags, small_sem,
-    field, level_bins, spread, taps, patches, part, mirror, total,
+    field, middle, level_bins, spread, taps, patches, part, mirror, total,
     load_sem, bins_send, bins_recv, halo_send, halo_recv, swap_send, swap_recv, out_send, out_recv,
 ):
     freq_count = surface.shape[1]
@@ -103,17 +103,24 @@
     has_down = strip < strips - 1
 
     field[...] = jnp.zeros_like(field)
+    level_bins[...] = jnp.full(level_bins.shape, -1, jnp.int32)
     first = pl.multiple_of(strip * ROWS, ROWS)
 
     def load_copy(c, place):
-        rows = (first, jnp.maximum(first - HALO, 0), jnp.minimum(first + ROWS, strips * ROWS - HALO))
-        size = (ROWS, HALO, HALO)[place]
-        target = (HALO, 0, HALO + ROWS)[place]
+        rows = (first, jnp.maximum(first - ROWS, 0), jnp.minimum(first + ROWS, (strips - 1) * ROWS))
+        target = (ROWS, 0, 2 * ROWS)[place]
         return pltpu.make_async_copy(
-            surface.at[0, :, :, pl.ds(pl.multiple_of(rows[place], HALO), size), pl.ds(c * width, width)],
-            field.at[0, :, :, c, pl.ds(target, size), :],
+            surface.at[0, :, :, pl.ds(pl.multiple_of(rows[place], ROWS), ROWS), pl.ds(c * width, width)],
+            field.at[0, :, :, c, pl.ds(target, ROWS), :],
             load_sem.at[c, place],
         )
+
+    def bins_places(target, level):
+        owner = snake(target % strips) * ROWS
+        start = jnp.clip(owner - HALO, 0, strips * ROWS - WINDOW)
+        source = pl.ds(pl.multiple_of(start, HALO), WINDOW)
+        place = pl.ds(pl.multiple_of(start - owner + ROWS, HALO), WINDOW)
+        return bins.at[0, source, :], level_bins.at[level, place, :]
 
     smalls = [
         pltpu.make_async_copy(far, near, small_sem.at[n])
@@ -124,7 +131,7 @@
     ]
     for small in smalls:
         small.start()
-    own_bins = pltpu.make_async_copy(bins.at[0, pl.ds(first, ROWS), :], level_bins.at[here], bins_send.at[0])
+    own_bins = pltpu.make_async_copy(*bins_places(here, here), bins_send.at[0])
     own_bins.start()
     for c in range(2):
         load_copy(c, 0).start()
@@ -146,7 +153,7 @@
     for small in smalls:
         small.wait()
     for f in range(freq_count):
-        patches[f, 3 * MAIN + 3 * WINDOW :, :] = jnp.zeros((WINDOW, PARTS * width), jnp.bfloat16)
+        patches[f, 3 * MAIN + 3 * WINDOW :, :] = jnp.zeros((WINDOW, 2 * PARTS * width), jnp.bfloat16)
         step = column(phase_step[f : f + 1, :], kernels)
         shift = column(phase_shift[f : f + 1, :], kernels)
         weights = [column(stencil[j, f : f + 1, :], kernels) for j in range(5)]
@@ -174,9 +181,9 @@
     pl.semaphore_wait(barrier, depth * freqs - 1)
 
     def bins_copy(target, level, sem):
-        rows = pl.ds(pl.multiple_of(snake(target % strips) * ROWS, ROWS), ROWS)
+        source, place = bins_places(target, level)
         return pltpu.make_async_remote_copy(
-            src_ref=bins.at[0, rows, :], dst_ref=level_bins.at[level],
+            src_ref=source, dst_ref=place,
             send_sem=bins_send.at[sem], recv_sem=bins_recv.at[level],
             device_id={"depth": target}, device_id_type=MESH,
         )
@@ -191,11 +198,10 @@
     down = group * strips + snake(jnp.minimum(strip + 1, strips - 1))
 
     def halo_copy(slot, f, way):
-        source = HALO if way == 0 else ROWS
-        target = HALO + ROWS if way == 0 else 0
+        target = 2 * ROWS if way == 0 else 0
         return pltpu.make_async_remote_copy(
-            src_ref=field.at[slot, f, :, :, pl.ds(source, HALO), :],
-            dst_ref=field.at[slot, f, :, :, pl.ds(target, HALO), :],
+            src_ref=field.at[slot, f, :, :, pl.ds(ROWS, ROWS), :],
+            dst_ref=field.at[slot, f, :, :, pl.ds(target, ROWS), :],
             send_sem=halo_send.at[way, slot, f], recv_sem=halo_recv.at[way, slot, f],
             device_id={"depth": up if way == 0 else down}, device_id_type=MESH,
         )
@@ -236,116 +242,142 @@
 
     def deliver_early(step, carry):
         index = (strip + step) % strips
-        pl.when(index < strips - 1)(lambda: deliver(index))
-        return carry
-
-    wide = lax.broadcasted_iota(jnp.int32, (WINDOW, width), 1)
+        pl.when(index < strips - 2)(lambda: deliver(index))
+        return carry
+
     lane = lax.broadcasted_iota(jnp.int32, (ROWS, width), 1)
 
-    def level(z, carry):
-        slot = z % 2
+    def apply(f, values, choice):
+        count = len(choice)
+        height = (count + 1) * ROWS
+        wide = lax.broadcasted_iota(jnp.int32, (height, width), 1)
+        for j in range(PARTS):
+            halves = split(values[j])
+            for b in range(TAPS):
+                reach = b - HALF
+                high, low = halves
+                if reach:
+                    inside = wide < width - reach if reach > 0 else wide >= -reach
+                    high, low = (
+                        jnp.where(inside, pltpu.roll(half, (-reach) % width, 1), jnp.zeros_like(half))
+                        for half in halves
+                    )
+                if b < TAPS - 1:
+                    places = [b * WINDOW + n * MAIN for n in range(3)]
+                else:
+                    places = [3 * MAIN + n * WINDOW for n in range(3)]
+                for n in range(count):
+                    cols = slice((n * PARTS + j) * width, (n * PARTS + j + 1) * width)
+                    for place, piece in zip(places, (high, low, high)):
+                        patches[f, place : place + WINDOW, cols] = piece[n * ROWS : n * ROWS + WINDOW]
+        result = jnp.dot(
+            taps[f], patches[f, :, : count * PARTS * width], preferred_element_type=jnp.float32
+        )
+        outcome = []
+        for n in range(count):
+            picked = [[jnp.zeros((ROWS, width), jnp.float32)] * PARTS for _ in range(2)]
+            for k in range(kernels):
+                mask = choice[n] == k
+                for c in range(2):
+                    rows = slice((2 * k + c) * ROWS, (2 * k + c + 1) * ROWS)
+                    picked[c] = [
+                        jnp.where(
+                            mask,
+                            result[rows, (n * PARTS + j) * width : (n * PARTS + j + 1) * width],
+                            picked[c][j],
+                        )
+                        for j in range(PARTS)
+                    ]
+            parts = []
+            for re in range(0, PARTS, 2):
+                parts.append(picked[0][re] - picked[1][re + 1])
+                parts.append(picked[0][re + 1] + picked[1][re])
+            outcome.append(parts)
+        return outcome
+
+    def correlate(index, read):
+        for n in range(lag_count):
+            lag = lags[n]
+            back = lax.rem(width - 2 * lag, width)
+            product = jnp.zeros((ROWS, width), jnp.float32)
+            for f in range(freq_count):
+                for j in range(2):
+                    product += read(f, 0, j) * pltpu.roll(read(f, 1, j), back, 1)
+            product = jnp.where(lane < width - 2 * lag, product, 0.0)
+            part[index, n] = pltpu.roll(product, lag, 1)
+        swap_copy(index).start()
+
+    def two_levels(step, carry):
+        z = 2 * step
+        slot = step % 2
         after = 1 - slot
         index = z - group * strips
 
         for f in range(freq_count):
             for way, has_send, has_recv in ((0, has_up, has_down), (1, has_down, has_up)):
 
-                @pl.when((z > 0) & has_recv)
+                @pl.when((step > 0) & has_recv)
                 def _():
                     halo_copy(slot, f, way).wait_recv()
 
-                @pl.when((z > 0) & has_send)
+                @pl.when((step > 0) & has_send)
                 def _():
                     halo_copy(slot, f, way).wait_send()
 
             if f == freq_count - 1:
-                pl.when((index >= 1) & (index <= strips))(lambda: collect(index - 1))
-
-                @pl.when(index == strips - 1)
+
+                @pl.when((index >= 2) & (index <= strips))
+                def _():
+                    collect(index - 2)
+                    collect(index - 1)
+
+                @pl.when(index == strips - 2)
                 def _():
                     lax.fori_loop(1, strips + 1, deliver_early, 0)
 
-                pl.when(index == strips)(lambda: deliver(strips - 1))
-
+                @pl.when(index == strips)
+                def _():
+                    deliver(strips - 2)
+                    deliver(strips - 1)
+
+            if f == 0:
+                for more in range(2):
+
+                    @pl.when(z + more != here)
+                    def _():
+                        bins_copy(here, z + more, 0).wait_recv()
+
+            choice = [
+                level_bins[z, pl.ds(HALO, ROWS), :], level_bins[z, pl.ds(HALO + ROWS, ROWS), :]
+            ]
+            outcome = apply(f, [field[slot, f, j // 2, j % 2] for j in range(PARTS)], choice)
+            for n in range(2):
+                for j in range(PARTS):
+                    middle[f, j // 2, j % 2, pl.ds(n * ROWS, ROWS), :] = outcome[n][j]
+            choice = [level_bins[z + 1, pl.ds(ROWS, ROWS), :]]
+            outcome = apply(f, [middle[f, j // 2, j % 2] for j in range(PARTS)], choice)
             for j in range(PARTS):
-                halves = split(field[slot, f, j // 2, j % 2])
-                cols = slice(j * width, (j + 1) * width)
-                for b in range(TAPS):
-                    reach = b - HALF
-                    high, low = halves
-                    if reach:
-                        inside = wide < width - reach if reach > 0 else wide >= -reach
-                        high, low = (
-                            jnp.where(inside, pltpu.roll(half, (-reach) % width, 1), jnp.zeros_like(half))
-                            for half in halves
-                        )
-                    if b < TAPS - 1:
-                        places = [b * WINDOW + n * MAIN for n in range(3)]
-                    else:
-                        places = [3 * MAIN + n * WINDOW for n in range(3)]
-                    for place, piece in zip(places, (high, low, high)):
-                        patches[f, place : place + WINDOW, cols] = piece
-            result = jnp.dot(taps[f], patches[f], preferred_element_type=jnp.float32)
-
-            if f == 0:
-
-                @pl.when(z != here)
-                def _():
-                    bins_copy(here, z, 0).wait_recv()
-
-            chosen = level_bins[z]
-            picked = None
-            for k in range(kernels):
-                rows = [
-                    [
-                        result[
-                            (2 * k + c) * ROWS : (2 * k + c + 1) * ROWS,
-                            j * width : (j + 1) * width,
-                        ]
-                        for j in range(PARTS)
-                    ]
-                    for c in range(2)
-                ]
-                if picked is None:
-                    picked = rows
-                else:
-                    mask = chosen == k
-                    picked = [
-                        [jnp.where(mask, rows[c][j], picked[c][j]) for j in range(PARTS)]
-                        for c in range(2)
-                    ]
-            for pair in range(PARTS // 2):
-                re, im = 2 * pair, 2 * pair + 1
-                field[after, f, pair, 0, pl.ds(HALO, ROWS), :] = picked[0][re] - picked[1][im]
-                field[after, f, pair, 1, pl.ds(HALO, ROWS), :] = picked[0][im] + picked[1][re]
+                field[after, f, j // 2, j % 2, pl.ds(ROWS, ROWS), :] = outcome[0][j]
 
             for way, has_send in ((0, has_up), (1, has_down)):
 
-                @pl.when((z < depth - 1) & has_send)
+                @pl.when((z < depth - 2) & has_send)
                 def _():
                     halo_copy(after, f, way).start()
 
         @pl.when((index >= 0) & (index < strips))
         def _():
-            for n in range(lag_count):
-                lag = lags[n]
-                back = lax.rem(width - 2 * lag, width)
-                product = jnp.zeros((ROWS, width), jnp.float32)
-                for f in range(freq_count):
-                    for j in range(PARTS // 2):
-                        source = field[after, f, 0, j, pl.ds(HALO, ROWS), :]
-                        receiver = field[after, f, 1, j, pl.ds(HALO, ROWS), :]
-                        product += source * pltpu.roll(receiver, back, 1)
-                product = jnp.where(lane < width - 2 * lag, product, 0.0)
-                part[index, n] = pltpu.roll(product, lag, 1)
-            swap_copy(index).start()
-
-        return carry
-
-    lax.fori_loop(0, depth, level, 0)
+            correlate(index, lambda f, pair, c: middle[f, pair, c, pl.ds(HALO, ROWS), :])
+            correlate(index + 1, lambda f, pair, c: field[after, f, pair, c, pl.ds(ROWS, ROWS), :])
+
+        return carry
+
+    lax.fori_loop(0, depth // 2, two_levels, 0)
 
     @pl.when(group == groups - 1)
     def _():
+        collect(strips - 2)
+        deliver(strips - 2)
         collect(strips - 1)
         deliver(strips - 1)
 
@@ -396,11 +428,12 @@
             pltpu.VMEM(phase_shift.shape, jnp.float32),
             pltpu.SMEM(lags.shape, jnp.int32),
             pltpu.SemaphoreType.DMA((4,)),
-            pltpu.VMEM((2, freq_count, PARTS // 2, 2, WINDOW, width), jnp.float32),
-            pltpu.VMEM((depth, ROWS, width), jnp.int32),
+            pltpu.VMEM((2, freq_count, PARTS // 2, 2, 3 * ROWS, width), jnp.float32),
+            pltpu.VMEM((freq_count, PARTS // 2, 2, WINDOW, width), jnp.float32),
+            pltpu.VMEM((depth, 3 * ROWS, width), jnp.int32),
             pltpu.VMEM((freq_count, tiles, 2 * kernels * ROWS, LANES), jnp.float32),
             pltpu.VMEM((freq_count, 2 * kernels * ROWS, CONTRACT), jnp.bfloat16),
-            pltpu.VMEM((freq_count, CONTRACT, PARTS * width), jnp.bfloat16),
+            pltpu.VMEM((freq_count, CONTRACT, 2 * PARTS * width), jnp.bfloat16),
             pltpu.VMEM((strips, lag_count, ROWS, width), jnp.float32),
             pltpu.VMEM((strips, share, ROWS, width), jnp.float32),
             pltpu.VMEM((strips, share, ROWS, width), jnp.float32),

time: 41.4 us -> 34.8 us (0.84)
  the two profiles are of different devices: /device:TPU:0 before, /device:TPU:27 now
where the time goes in v4:
time: 34.8 us; the launch traced here: 34.6 us
  Pallas kernels  33 us (95%)
  local copies, waits for them, and re-layouts  1.61 us (5%)
    pallas_call x1, Pallas kernels, body(): pl.pallas_call(functools.partial(kernel, depth, groups, freqs), out_shape...  33 us
    reshape x1, local copies, waits for them, and re-layouts, body(): return image.reshape(1, lag_count, per_core * ROWS * width)  1.61 us

profile of v4, /device:TPU:27, one launch (start us, length us, event | category | flops | bytes accessed | tf_op | source)
XLA Modules:
  0.0 34.6 jit_solution(8665821641967616599)
XLA Ops:
  0.0 33.0 %shard_map.64 = f32[4,64,128]{2,1,0:T(8,128)} custom-call(f32[1,2,2,128,256]{4,3,2,1,0:T(8,128)} %surface.1, s32[1,128,128]{2,1,0:T(8,128)} %bins.1, f32[5,2,8]{2,1,0:T(2,128)} %bitcast.1, f32[2,8]{1,0:T(2,128)} %phase_step_far.1, f32[2,8]{1,0:T(2,128)} %phase_shift_far.1, s32[4]{0:T(128)} %lags_far.1), custom_call_target="tpu_custom_call" | custom-call | flops 5368709120 | bytes 1048576 | tf_op jit(solution)/shard_map/pallas_call | solution.py:420
  33.0 1.6 %reshape.3 = f32[1,4,8192]{2,1,0:T(4,128)} reshape(f32[4,64,128]{2,1,0:T(8,128)} %shard_map.64) | data formatting | bytes 262144 | tf_op jit(solution)/shard_map/reshape | solution.py:455

commit v5 on v4

--- a/solution.py
+++ b/solution.py
@@ -26,19 +26,11 @@
     return 2 * pair + (index % 2 + pair % 2) % 2
 
 
-def column(row_values, count):
-    rows = lax.broadcasted_iota(jnp.int32, (count, count), 0)
-    cols = lax.broadcasted_iota(jnp.int32, (count, count), 1)
-    spread = jnp.broadcast_to(row_values, (count, count))
-    return jnp.sum(jnp.where(rows == cols, spread, 0.0), axis=1, keepdims=True)
-
-
 def build_taps(weights, step, shift, kernels):
     center, along_x, along_y, main, anti = weights
     scale = step / (center + 2.0 * (along_x + along_y + main + anti))
     center, along_x, along_y, main, anti = (
-        jnp.broadcast_to(part * scale, (kernels, LANES))
-        for part in (center, along_x, along_y, main, anti)
+        part * scale for part in (center, along_x, along_y, main, anti)
     )
     lane = lax.broadcasted_iota(jnp.int32, (kernels, LANES), 1)
     tiles = -(-TAPS // PER_TILE)
@@ -68,8 +60,7 @@
         target = imag if order % 2 else real
         for t in range(tiles):
             target[t] = target[t] + power[t] * factor
-    cosine = jnp.broadcast_to(jnp.cos(shift), (kernels, LANES))
-    sine = jnp.broadcast_to(jnp.sin(shift), (kernels, LANES))
+    cosine, sine = jnp.cos(shift), jnp.sin(shift)
     kern_real = [cosine * r - sine * i for r, i in zip(real, imag)]
     kern_imag = [sine * r + cosine * i for r, i in zip(real, imag)]
     return kern_real, kern_imag
@@ -84,7 +75,7 @@
 def kernel(
     depth, groups, freqs,
     surface, bins, stencil_far, phase_step_far, phase_shift_far, lags_far, out,
-    stencil, phase_step, phase_shift, lags, small_sem,
+    got, stencil, phase_step, phase_shift, lags, small_sem,
     field, middle, level_bins, spread, taps, patches, part, mirror, total,
     load_sem, bins_send, bins_recv, halo_send, halo_recv, swap_send, swap_recv, out_send, out_recv,
 ):
@@ -152,16 +143,47 @@
 
     for small in smalls:
         small.wait()
+    def column(values):
+        shape = (kernels, LANES)
+        rows = lax.broadcasted_iota(jnp.int32, (kernels, kernels), 0)
+        cols = lax.broadcasted_iota(jnp.int32, (kernels, kernels), 1)
+        pieces = []
+        for f in range(freq_count):
+            wide = jnp.broadcast_to(values[f : f + 1, :], (kernels, kernels))
+            narrow = jnp.sum(jnp.where(rows == cols, wide, 0.0), axis=1, keepdims=True)
+            pieces.append(jnp.broadcast_to(narrow, shape))
+        return jnp.concatenate(pieces, axis=0)
+
+    kern = build_taps(
+        [column(stencil[j]) for j in range(5)], column(phase_step[...]), column(phase_shift[...]),
+        freq_count * kernels,
+    )
+
+    own_bins.wait()
+    pl.semaphore_wait(barrier, depth * freqs - 1)
+
+    def bins_copy(target, level, sem):
+        source, place = bins_places(target, level)
+        return pltpu.make_async_remote_copy(
+            src_ref=source, dst_ref=place,
+            send_sem=bins_send.at[sem], recv_sem=bins_recv.at[level],
+            device_id={"depth": target}, device_id_type=MESH,
+        )
+
+    def send_bins(step, carry):
+        bins_copy((here + step) % depth, here, step).start()
+        return carry
+
+    lax.fori_loop(1, depth, send_bins, 0)
+
     for f in range(freq_count):
         patches[f, 3 * MAIN + 3 * WINDOW :, :] = jnp.zeros((WINDOW, 2 * PARTS * width), jnp.bfloat16)
-        step = column(phase_step[f : f + 1, :], kernels)
-        shift = column(phase_shift[f : f + 1, :], kernels)
-        weights = [column(stencil[j, f : f + 1, :], kernels) for j in range(5)]
-        kern = build_taps(weights, step, shift, kernels)
         for c in range(2):
             for t in range(len(kern[c])):
                 for y in range(ROWS):
-                    moved = pltpu.roll(kern[c][t], y, 1) if y else kern[c][t]
+                    moved = kern[c][t][f * kernels : (f + 1) * kernels]
+                    if y:
+                        moved = pltpu.roll(moved, y, 1)
                     spread[f, t, pl.ds(c * ROWS + y, kernels, stride=2 * ROWS), :] = moved
         for t in range(MAIN // LANES):
             high, low = split(spread[f, t])
@@ -173,26 +195,10 @@
         last = high + pltpu.roll(high, WINDOW, 1) + pltpu.roll(low, 2 * WINDOW, 1)
         taps[f, :, 3 * MAIN :] = last.astype(jnp.bfloat16)
 
-    own_bins.wait()
     for c in range(2):
         load_copy(c, 0).wait()
         pl.when(has_up)(load_copy(c, 1).wait)
         pl.when(has_down)(load_copy(c, 2).wait)
-    pl.semaphore_wait(barrier, depth * freqs - 1)
-
-    def bins_copy(target, level, sem):
-        source, place = bins_places(target, level)
-        return pltpu.make_async_remote_copy(
-            src_ref=source, dst_ref=place,
-            send_sem=bins_send.at[sem], recv_sem=bins_recv.at[level],
-            device_id={"depth": target}, device_id_type=MESH,
-        )
-
-    def send_bins(step, carry):
-        bins_copy((here + step) % depth, here, step).start()
-        return carry
-
-    lax.fori_loop(1, depth, send_bins, 0)
 
     up = group * strips + snake(jnp.maximum(strip - 1, 0))
     down = group * strips + snake(jnp.minimum(strip + 1, strips - 1))
@@ -218,7 +224,7 @@
     def out_copy(index, from_core, from_place):
         rows = pl.ds(pl.multiple_of(from_place * ROWS, ROWS), ROWS)
         return pltpu.make_async_remote_copy(
-            src_ref=total.at[index], dst_ref=out.at[pl.ds(from_core * share, share), rows, :],
+            src_ref=total.at[index], dst_ref=got.at[pl.ds(from_core * share, share), rows, :],
             send_sem=out_send.at[index], recv_sem=out_recv.at[from_core, from_place],
             device_id={"depth": group * strips + index, "freq": out_core}, device_id_type=MESH,
         )
@@ -234,7 +240,7 @@
         @pl.when(owned(index))
         def _():
             rows = pl.ds(pl.multiple_of(strip % per_core * ROWS, ROWS), ROWS)
-            out[pl.ds(core * share, share), rows, :] = total[index]
+            got[pl.ds(core * share, share), rows, :] = total[index]
 
         @pl.when(jnp.logical_not(owned(index)))
         def _():
@@ -247,8 +253,8 @@
 
     lane = lax.broadcasted_iota(jnp.int32, (ROWS, width), 1)
 
-    def apply(f, values, choice):
-        count = len(choice)
+    def apply(f, values, z, places):
+        count = len(places)
         height = (count + 1) * ROWS
         wide = lax.broadcasted_iota(jnp.int32, (height, width), 1)
         for j in range(PARTS):
@@ -263,16 +269,23 @@
                         for half in halves
                     )
                 if b < TAPS - 1:
-                    places = [b * WINDOW + n * MAIN for n in range(3)]
+                    spots = [b * WINDOW + n * MAIN for n in range(3)]
                 else:
-                    places = [3 * MAIN + n * WINDOW for n in range(3)]
+                    spots = [3 * MAIN + n * WINDOW for n in range(3)]
                 for n in range(count):
                     cols = slice((n * PARTS + j) * width, (n * PARTS + j + 1) * width)
-                    for place, piece in zip(places, (high, low, high)):
-                        patches[f, place : place + WINDOW, cols] = piece[n * ROWS : n * ROWS + WINDOW]
+                    for spot, piece in zip(spots, (high, low, high)):
+                        patches[f, spot : spot + WINDOW, cols] = piece[n * ROWS : n * ROWS + WINDOW]
         result = jnp.dot(
             taps[f], patches[f, :, : count * PARTS * width], preferred_element_type=jnp.float32
         )
+        if f == 0:
+
+            @pl.when(z != here)
+            def _():
+                bins_copy(here, z, 0).wait_recv()
+
+        choice = [level_bins[z, pl.ds(place, ROWS), :] for place in places]
         outcome = []
         for n in range(count):
             picked = [[jnp.zeros((ROWS, width), jnp.float32)] * PARTS for _ in range(2)]
@@ -340,22 +353,20 @@
                     deliver(strips - 2)
                     deliver(strips - 1)
 
-            if f == 0:
-                for more in range(2):
-
-                    @pl.when(z + more != here)
-                    def _():
-                        bins_copy(here, z + more, 0).wait_recv()
-
-            choice = [
-                level_bins[z, pl.ds(HALO, ROWS), :], level_bins[z, pl.ds(HALO + ROWS, ROWS), :]
-            ]
-            outcome = apply(f, [field[slot, f, j // 2, j % 2] for j in range(PARTS)], choice)
+            values = [field[slot, f, j // 2, j % 2] for j in range(PARTS)]
+            outcome = apply(f, values, z, (HALO, HALO + ROWS))
             for n in range(2):
                 for j in range(PARTS):
                     middle[f, j // 2, j % 2, pl.ds(n * ROWS, ROWS), :] = outcome[n][j]
-            choice = [level_bins[z + 1, pl.ds(ROWS, ROWS), :]]
-            outcome = apply(f, [middle[f, j // 2, j % 2] for j in range(PARTS)], choice)
+
+            if f == freq_count - 1:
+
+                @pl.when((index >= 0) & (index < strips))
+                def _():
+                    correlate(index, lambda g, pair, c: middle[g, pair, c, pl.ds(HALO, ROWS), :])
+
+            values = [middle[f, j // 2, j % 2] for j in range(PARTS)]
+            outcome = apply(f, values, z + 1, (ROWS,))
             for j in range(PARTS):
                 field[after, f, j // 2, j % 2, pl.ds(ROWS, ROWS), :] = outcome[0][j]
 
@@ -367,7 +378,6 @@
 
         @pl.when((index >= 0) & (index < strips))
         def _():
-            correlate(index, lambda f, pair, c: middle[f, pair, c, pl.ds(HALO, ROWS), :])
             correlate(index + 1, lambda f, pair, c: field[after, f, pair, c, pl.ds(ROWS, ROWS), :])
 
         return carry
@@ -400,6 +410,8 @@
             def _():
                 out_copy(0, from_core, place).wait_recv()
 
+    for row in range(per_core * ROWS):
+        out[0, :, row * width : (row + 1) * width] = got[:, row, :]
     lax.fori_loop(0, strips, finish_out, 0)
     lax.fori_loop(1, depth, finish_bins, 0)
 
@@ -417,12 +429,13 @@
     tiles = -(-TAPS // PER_TILE)
     cost = 2 * freq_count * depth * 2 * kernels * ROWS * CONTRACT * PARTS * width
     vmem = pl.BlockSpec(memory_space=pltpu.VMEM)
-    image = pl.pallas_call(
+    return pl.pallas_call(
         functools.partial(kernel, depth, groups, freqs),
-        out_shape=jax.ShapeDtypeStruct((lag_count, per_core * ROWS, width), jnp.float32),
+        out_shape=jax.ShapeDtypeStruct((1, lag_count, per_core * ROWS * width), jnp.float32),
         in_specs=[pl.BlockSpec(memory_space=pl.ANY)] * 6,
         out_specs=vmem,
         scratch_shapes=[
+            pltpu.VMEM((lag_count, per_core * ROWS, width), jnp.float32),
             pltpu.VMEM((stencil.shape[2], freq_count, kernels), jnp.float32),
             pltpu.VMEM(phase_step.shape, jnp.float32),
             pltpu.VMEM(phase_shift.shape, jnp.float32),
@@ -452,7 +465,6 @@
         ),
         cost_estimate=pl.CostEstimate(flops=cost, bytes_accessed=1 << 20, transcendentals=0),
     )(surface, bins, jnp.transpose(stencil, (2, 0, 1)), phase_step, phase_shift, lags)
-    return image.reshape(1, lag_count, per_core * ROWS * width)
 
 
 def solution(mesh):

time: 34.8 us -> 34.7 us (level)
  the two profiles are of different devices: /device:TPU:27 before, /device:TPU:0 now
where the time goes in v5:
time: 34.7 us; the launch traced here: 34.5 us
  Pallas kernels  32.9 us (95%)
  local copies, waits for them, and re-layouts  1.57 us (5%)
    pallas_call x1, Pallas kernels, body(): pl.pallas_call(functools.partial(kernel, depth, groups, freqs), out_shape...  32.9 us
    unnamed x1, local copies, waits for them, and re-layouts  1.57 us

profile of v5, /device:TPU:0, one launch (start us, length us, event | category | flops | bytes accessed | tf_op | source)
XLA Modules:
  0.0 34.5 jit_solution(17844608864542965720)
XLA Ops:
  0.0 32.9 %shard_map.64 = f32[1,4,8192]{2,1,0:T(4,128)} custom-call(f32[1,2,2,128,256]{4,3,2,1,0:T(8,128)} %surface.1, s32[1,128,128]{2,1,0:T(8,128)} %bins.1, f32[5,2,8]{2,1,0:T(2,128)} %bitcast.1, f32[2,8]{1,0:T(2,128)} %phase_step_far.1, f32[2,8]{1,0:T(2,128)} %phase_shift_far.1, s32[4]{0:T(128)} %lags_far.1), custom_call_target="tpu_custom_call" | custom-call | flops 5368709120 | bytes 1048576 | tf_op jit(solution)/shard_map/pallas_call | solution.py:432
  32.9 1.6 %copy.8 = f32[1,4,8192]{2,1,0:T(4,128)} copy(f32[1,4,8192]{2,1,0:T(4,128)} %shard_map.64) | data formatting | bytes 262144
